TPU v7x, 32 devices: a whole 2x2x4 slice. The times are simulated.
32 devices in a mesh: groups: 2 (over y), replica: 4 (over z), tensor: 4 (over x, core).
Axes of the slice: x: 2, y: 2, z: 4, core: 2. Of those that a mesh axis runs over, the one named last changes fastest.
Arguments:
- normed_hidden_rows: bfloat16 [1024, 8192], P(('groups', 'replica')), parts along dimension 0, may hold values from -6 to 6
- queries: bfloat16 [1024, 64, 128], P(('groups', 'replica'), 'tensor'), parts along dimension 0, may hold values from -8 to 8
- incoming_key: bfloat16 [1024, 8, 128], P(('groups', 'replica'), 'tensor'), parts along dimension 0, may hold values from -5 to 5
- stored_key_cache: bfloat16 [1024, 64, 8, 128], P(('groups', 'replica'), None, 'tensor'), parts along dimension 0, may hold values from -5 to 5
- stored_value_cache: bfloat16 [1024, 64, 8, 128], P(('groups', 'replica'), None, 'tensor'), parts along dimension 0, may hold values from -6 to 6
- value_weight: bfloat16 [8192, 1024], P(None, 'tensor'), may hold values from -0.0625 to 0.0625
- adapter_down_weight: bfloat16 [16, 64, 8192], P('replica', None, 'tensor'), may hold values from -0.0625 to 0.0625
- adapter_up_weight: bfloat16 [16, 64, 1024], P('replica', None, 'tensor'), may hold values from -0.75 to 0.75
- token_adapter_index: int32 [1024], P(('groups', 'replica')), parts along dimension 0, may hold values from 0 to 15, as said below
- adapter_holder_replica: int32 [32], P('groups'), parts along dimension 0, may hold values from 0 to 3, as said below
- refill: int32 [1024], P(('groups', 'replica')), parts along dimension 0, may hold values 0 or 1
Outputs:
- incoming_value: bfloat16 [1024, 1024], P(('groups', 'replica'), 'tensor'), parts along dimension 0
- attended: bfloat16 [1024, 8192], P(('groups', 'replica'), 'tensor'), parts along dimension 0
There are 2 independent parts, one for each index of `groups`. A program takes and returns all parts, laid end to end along the dimension named above; an argument that names none is the same for every part. Nothing has to cross between parts.
Inputs may be any that keep to these rules, and one draw needn't show every extreme that they name: `adapter_holder_replica`: every replica index owns exactly 4 adapters. `token_adapter_index`: among the 128 tokens of one replica (tokens 128*r to 128*r + 127), at most 32 use adapters owned by one replica; some replica owns the adapters of exactly 32 tokens of every replica.
All inputs are finite; a program needn't handle non-finite values. No bound on the sum of `refill` on one device may be relied on, other than what follows from the above.
Results may differ from a plain program's by a relative error of at most 0.0055.
Values may be sent and summed in bfloat16 or wider, within the bound.
No kernel may reach another device: no remote copies, remote signals or barrier semaphores. Data moves between devices by JAX's collectives and lax.ppermute only.
A program may use at most 64 MiB of HBM per device.

v0:
```python
import jax
import jax.numpy as jnp
from jax import lax
from jax.sharding import PartitionSpec as P

adapter_output_scale = 0.5
mask_value = -1e30


def adapter_store_slots(adapter_holder_replica, per_owner):
    count_all = adapter_holder_replica.shape[0]
    row_order = jnp.arange(count_all, dtype=jnp.int32)
    earlier = (adapter_holder_replica[:, None] == adapter_holder_replica[None, :]) & (
        row_order[None, :] < row_order[:, None]
    )
    return adapter_holder_replica * per_owner + jnp.sum(earlier.astype(jnp.int32), axis=1)


def lookup(small_table, indices):
    matches = indices[:, None] == jnp.arange(small_table.shape[0], dtype=jnp.int32)[None, :]
    return jnp.sum(jnp.where(matches, small_table[None, :], 0), axis=1)


def holder_shrink_output(batch_row_input, batch_row_slots, adapter_down_weight):
    leading_slot = lax.axis_index("replica") * adapter_down_weight.shape[0]
    replica_local_slots = leading_slot + jnp.arange(adapter_down_weight.shape[0], dtype=jnp.int32)
    holder_mask = batch_row_slots[None, :] == replica_local_slots[:, None]
    value_projected = jnp.einsum(
        "ek,cyk->cey", batch_row_input, adapter_down_weight, preferred_element_type=jnp.float32
    )
    partial_value = jnp.sum(jnp.where(holder_mask[:, :, None], value_projected, 0.0), axis=0)
    summed = lax.psum(partial_value, "tensor")
    return (summed.astype(jnp.bfloat16), holder_mask)


def holder_expand_output(shrink_output, holder_mask, adapter_up_weight):
    expanded_output = jnp.einsum(
        "tv,wvl->wtl", shrink_output, adapter_up_weight, preferred_element_type=jnp.float32
    )
    return adapter_output_scale * jnp.sum(
        jnp.where(holder_mask[:, :, None], expanded_output, 0.0), axis=0
    )


def body(
    normed_hidden_rows,
    queries,
    incoming_key,
    stored_key_cache,
    stored_value_cache,
    value_weight,
    adapter_down_weight,
    adapter_up_weight,
    token_adapter_index,
    adapter_holder_replica,
    refill,
):
    row_count = normed_hidden_rows.shape[0]
    slice_column_width = adapter_down_weight.shape[2]
    x_slice = lax.dynamic_slice_in_dim(
        normed_hidden_rows, lax.axis_index("tensor") * slice_column_width, slice_column_width, 1
    )
    slot_table = adapter_store_slots(adapter_holder_replica, adapter_down_weight.shape[0])
    token_row_slot = lookup(slot_table, token_adapter_index)
    base_value_output = jnp.dot(
        normed_hidden_rows, value_weight, preferred_element_type=jnp.float32
    )
    collected_input, collected_slot = (
        lax.all_gather(x_slice, "replica", axis=0, tiled=True),
        lax.all_gather(token_row_slot, "replica", axis=0, tiled=True),
    )
    shrink_output, holder_mask = holder_shrink_output(
        collected_input, collected_slot, adapter_down_weight
    )
    adapter_delta = lax.psum_scatter(
        holder_expand_output(shrink_output, holder_mask, adapter_up_weight),
        "replica",
        scatter_dimension=0,
        tiled=True,
    )
    incoming_value = (base_value_output + adapter_delta).astype(jnp.bfloat16)
    local_heads = queries.shape[1]
    head_size = queries.shape[2]
    local_kv = incoming_key.shape[1]
    group_size = local_heads // local_kv
    score_scale = head_size ** (-0.5)
    grouped = queries.reshape(row_count, local_kv, group_size, head_size)
    scores = (
        jnp.einsum("rkgd,rckd->rkgc", grouped, stored_key_cache, preferred_element_type=jnp.float32)
        * score_scale
    )
    scores = jnp.where(refill[:, None, None, None] == 1, mask_value, scores)
    fresh_score = (
        jnp.einsum("rkgd,rkd->rkg", grouped, incoming_key, preferred_element_type=jnp.float32)
        * score_scale
    )
    row_top = jnp.maximum(jnp.max(scores, axis=-1), fresh_score)
    cache_exp = jnp.exp(scores - row_top[..., None])
    fresh_exp = jnp.exp(fresh_score - row_top)
    denominator = jnp.sum(cache_exp, axis=-1) + fresh_exp
    cache_weight = (cache_exp / denominator[..., None]).astype(jnp.bfloat16)
    fresh_weight = (fresh_exp / denominator).astype(jnp.bfloat16)
    output = jnp.einsum(
        "rkgc,rckd->rkgd", cache_weight, stored_value_cache, preferred_element_type=jnp.float32
    )
    value_heads = incoming_value.reshape(row_count, local_kv, head_size).astype(jnp.float32)
    output = output + fresh_weight.astype(jnp.float32)[..., None] * value_heads[:, :, None, :]
    attended = output.reshape(row_count, local_heads * head_size).astype(jnp.bfloat16)
    return (incoming_value, attended)


def solution(mesh):
    return jax.shard_map(
        body,
        mesh=mesh,
        in_specs=(
            P(("groups", "replica"), None),
            P(("groups", "replica"), "tensor", None),
            P(("groups", "replica"), "tensor", None),
            P(("groups", "replica"), None, "tensor", None),
            P(("groups", "replica"), None, "tensor", None),
            P(None, "tensor"),
            P("replica", None, "tensor"),
            P("replica", None, "tensor"),
            P(("groups", "replica")),
            P("groups"),
            P(("groups", "replica")),
        ),
        out_specs=(P(("groups", "replica"), "tensor"), P(("groups", "replica"), "tensor")),
        check_vma=False,
    )
```

profile of v0, /device:TPU:0, one launch (start us, length us, event | category | flops | bytes accessed | tf_op | source)
XLA Modules:
  0.0 109.6 jit_solution(7247396944606640577)
XLA Ops:
  7.2 1.5 %copy-done = bf16[128,8192]{1,0:T(8,128)(2,1)S(1)} copy-done((bf16[128,8192]{1,0:T(8,128)(2,1)S(1)}, bf16[128,8192]{1,0:T(8,128)(2,1)}, u32[]{:S(2)}) %copy-start) | copy-done | bytes 2097176
  8.8 0.8 constant_dynamic-slice_fusion
  9.7 0.9 convert_reduce_fusion
  10.6 0.7 multiply_add_fusion
  11.3 0.7 select_reduce_fusion
  12.0 12.6 %all-gather = s32[4,1,128]{2,1,0:T(1,128)S(1)} all-gather(s32[1,1,128]{2,1,0:T(1,128)S(1)} %bitcast.60), channel_id=1, replica_groups=mesh['groups'=2,'replica'=4,'tensor'=4] {'replica'}, dimensions={0}, use_global_device_ids=true | all-gather | bytes 2560 | tf_op jit(solution)/shard_map/all_gather | solution.py:70
  24.6 0.7 broadcast_compare_fusion.1
  25.3 0.1 broadcast_compare_fusion
  25.4 33.5 %all-gather.3.cloned.1.call-done = bf16[512,2048]{1,0:T(8,128)(2,1)} async-done(((bf16[128,2048]{1,0:T(8,128)(2,1)}), bf16[512,2048]{1,0:T(8,128)(2,1)}) %all-gather.3.cloned.1.call-update) | async-done | bytes 2097168 | tf_op jit(solution)/shard_map/all_gather | solution.py:69
  58.8 2.6 %fusion.25 = f32[512,64]{0,1:T(8,128)S(1)} fusion(bf16[4,64,2048]{2,1,0:T(8,128)(2,1)} %param.17, bf16[512,2048]{1,0:T(8,128)(2,1)} %all-gather.3.cloned.1.call-done, pred[4,512]{1,0:T(4,128)(4,1)S(1)} %broadcast_compare_fusion), kind=kOutput, calls=%fused_computation.14 | convolution fusion | flops 537100288 | bytes 3278848 | tf_op jit(solution)/shard_map/ek,cyk->cey/dot_general | solution.py:28
  61.5 13.0 %all-reduce.1 = bf16[512,64]{0,1:T(8,128)(2,1)S(1)} all-reduce(f32[512,64]{0,1:T(8,128)S(1)} %fusion.25), channel_id=1, replica_groups=mesh['groups'=2,'replica'=4,'tensor'=4] {'tensor'}, use_global_device_ids=true, to_apply=%region_3.4 | all-reduce | flops 32768 | bytes 196608 | tf_op jit(solution)/shard_map/psum | solution.py:32
  74.4 0.5 fusion.4
  74.9 0.8 broadcast_multiply_fusion
  75.8 4.8 %fusion.42 = (f32[128,2,8]{2,1,0:T(2,128)S(1)}, f32[128,2,8,64]{3,2,1,0:T(8,128)S(1)}) fusion(bf16[128,64,2,128]{3,2,1,0:T(2,128)(2,1)} %param.14, bf16[128,16,128]{2,1,0:T(8,128)(2,1)} %param.12, pred[128]{0:T(512)(128)(4,1)S(1)} %broadcast_compare_fusion.1), kind=kOutput, calls=%fused_computation.46 | convolution fusion | flops 33945600 | bytes 5251200 | tf_op jit(solution)/shard_map/rkgd,rckd->rkgc/dot_general | solution.py:89
  80.6 1.5 %fusion.30 = f32[128,2,1,8]{3,2,1,0:T(1,128)S(1)} fusion(bf16[128,16,128]{2,1,0:T(8,128)(2,1)} %param.12, bf16[128,2,128,1]{2,1,0,3:T(2,128)(2,1)S(1)} %bitcast.61), kind=kOutput, calls=%fused_computation.21 | convolution fusion | flops 524288 | bytes 598016 | tf_op jit(solution)/shard_map/rkgd,rkd->rkg/dot_general | solution.py:94
  82.2 0.2 copy.26
  82.4 0.8 fusion.29
  83.2 0.8 copy.28
  84.0 0.8 copy.30
  84.8 10.5 %reduce-scatter.2.cloned.1.call-done = f32[128,256]{1,0:T(8,128)} async-done(((f32[512,256]{1,0:T(8,128)}), f32[128,256]{1,0:T(8,128)}) %reduce-scatter.2.cloned.1.call-update) | async-done | bytes 131088 | tf_op jit(solution)/shard_map/reduce_scatter | solution.py:75
  95.3 2.9 %fusion.28 = bf16[128,256]{1,0:T(8,128)(2,1)S(1)} fusion(f32[128,256]{1,0:T(8,128)} %reduce-scatter.2.cloned.1.call-done, bf16[128,8192]{1,0:T(8,128)(2,1)S(1)} %copy-done, bf16[8192,256]{1,0:T(8,128)(2,1)} %param.16), kind=kOutput, calls=%fused_computation.16 | convolution fusion | flops 536936448 | bytes 6488064 | tf_op jit(solution)/shard_map/dot_general | solution.py:65
  98.3 0.1 reshape.57
  98.3 3.5 %fusion.16 = bf16[128,2,8,128]{3,2,1,0:T(8,128)(2,1)S(1)} fusion(bf16[128,64,2,128]{3,2,1,0:T(2,128)(2,1)} %param.15, f32[128,2,8,64]{3,2,1,0:T(8,128)S(1)} %get-tuple-element.5, f32[128,2,128]{2,1,0:T(2,128)S(1)} %reshape.57, f32[128,2,8]{2,1,0:T(2,128)} %copy.30, f32[128,2,8]{2,1,0:T(2,128)} %copy.28, f32[128,2,8]{2,1,0:T(2,128)S(1)} %copy.26), kind=kOutput, calls=%fused_computation.11 | convolution fusion | flops 34734080 | bytes 5398528 | tf_op jit(solution)/shard_map/rkgc,rckd->rkgd/dot_general | solution.py:103
  101.8 0.9 copy.51
  (17 shorter events, 0.4 us)
Async XLA Ops:
  7.2 1.6 %copy-start = (bf16[128,8192]{1,0:T(8,128)(2,1)S(1)}, bf16[128,8192]{1,0:T(8,128)(2,1)}, u32[]{:S(2)}) copy-start(bf16[128,8192]{1,0:T(8,128)(2,1)} %param.11) | copy-start | bytes 6291460
  7.2 67.3 %copy-start.2 = (bf16[4,64,256]{2,1,0:T(8,128)(2,1)S(1)}, bf16[4,64,256]{2,1,0:T(8,128)(2,1)}, u32[]{:S(2)}) copy-start(bf16[4,64,256]{2,1,0:T(8,128)(2,1)} %param.18) | copy-start | bytes 393220
  7.2 51.7 %all-gather.3.cloned.1.call-start = ((), (), s32[]{:S(2)}) async-start(), calls=%async_computation.1 | async-start | bytes 2621440 | tf_op jit(solution)/shard_map/all_gather | solution.py:69
  9.6 85.7 %reduce-scatter.2.cloned.1.call-start = ((), (), s32[]{:S(2)}) async-start(), calls=%async_computation.2 | async-start | bytes 655360 | tf_op jit(solution)/shard_map/reduce_scatter | solution.py:75
  74.9 5.7 %copy-start.3 = (bf16[128,2,128]{2,1,0:T(2,128)(2,1)S(1)}, bf16[128,2,128]{2,1,0:T(2,128)(2,1)}, u32[]{:S(2)}) copy-start(bf16[128,2,128]{2,1,0:T(2,128)(2,1)} %param.13) | copy-start | bytes 196612
  98.3 3.6 %copy-start.1 = (bf16[128,256]{1,0:T(8,128)(2,1)}, bf16[128,256]{1,0:T(8,128)(2,1)S(1)}, u32[]{:S(2)}) copy-start(bf16[128,256]{1,0:T(8,128)(2,1)S(1)} %fusion.28) | copy-start | bytes 196612
Sparse Core Ops, SparseCore 0:
  10.2 48.6 all-gather.2
  75.9 19.3 reduce-scatter.1
where the time goes:
time: 110 us
  waiting for transfers between devices  44 us (40%)
  blocking collectives  25.6 us (23%)
  matrix products  15.7 us (14%)
  between operations  14.2 us (13%)
  local copies, waits for them, and re-layouts  5.31 us (5%)
  other arithmetic  4.68 us (4%)
    all_gather x1, waiting for transfers between devices, body(): lax.all_gather(x_slice, 'replica', axis=0, tiled=True)  33.5 us
    psum x1, blocking collectives, holder_shrink_output(): summed = lax.psum(partial_value, 'tensor')  13 us
    all_gather x1, blocking collectives, body(): lax.all_gather(token_row_slot, 'replica', axis=0, tiled=True)  12.6 us
    reduce_scatter x1, waiting for transfers between devices, body(): lax.psum_scatter(holder_expand_output(shrink_output, holder_mask, adapter...  10.5 us
    dot_general x1, matrix products, body(): jnp.einsum('rkgd,rckd->rkgc', grouped, stored_key_cache, preferred_elemen...  4.79 us
    dot_general x1, matrix products, body(): jnp.einsum('rkgc,rckd->rkgd', cache_weight, stored_value_cache, preferred...  3.47 us
    dot_general x1, matrix products, body(): jnp.dot(normed_hidden_rows, value_weight, preferred_element_type=jnp.floa...  2.9 us
    dot_general x1, matrix products, holder_shrink_output(): jnp.einsum('ek,cyk->cey', batch_row_input, adapter_down_weight, preferred...  2.62 us
  transfers between devices with their start and end apart: 2, of which 2 were waited for; matrix products, arithmetic and copies ran while one was open for 11% of the time, Pallas kernels for 0%

commit v1 on v0

v1 whole, which is shorter than its diff:
```python
import functools

import jax
import jax.numpy as jnp
from jax import lax
from jax.experimental import pallas as pl
from jax.experimental.pallas import tpu as pltpu
from jax.sharding import PartitionSpec as P

adapter_output_scale = 0.5
mask_value = -1e30
LANES = 128
VMEM = pl.BlockSpec(memory_space=pltpu.VMEM)
ANY = pl.BlockSpec(memory_space=pl.ANY)
F32 = jnp.float32
BF16 = jnp.bfloat16


def iota(shape, dimension):
    return lax.broadcasted_iota(jnp.int32, shape, dimension)


def to_column(row):
    size = row.shape[1]
    eye = iota((size, size), 0) == iota((size, size), 1)
    return jnp.sum(jnp.where(eye, row, 0.0), axis=1, keepdims=True)


def partner_pairs(replicas, step):
    if replicas & (replicas - 1) == 0:
        return [(r, r ^ step) for r in range(replicas)]
    return [(r, (r + step) % replicas) for r in range(replicas)]


def return_pairs(replicas, step):
    return [(b, a) for a, b in partner_pairs(replicas, step)]


def route_kernel(replicas, block, tokens_ref, holder_ref, x_ref, *refs):
    messages, order_ref, x_buf, sems = refs[:replicas], refs[replicas], refs[-2], refs[-1]
    rows, width = x_buf.shape
    pieces = sems.shape[0]
    piece = width // pieces
    first = lax.axis_index("tensor") * width
    copies = [
        pltpu.make_async_copy(
            x_ref.at[:, pl.ds(pl.multiple_of(first + i * piece, LANES), piece)],
            x_buf.at[:, pl.ds(i * piece, piece)],
            sems.at[i],
        )
        for i in range(pieces)
    ]
    for copy in copies:
        copy.start()
    me = lax.axis_index("replica")
    adapters = holder_ref.shape[1]
    holder_row = holder_ref[...].astype(F32)
    holder_col = to_column(holder_row)
    earlier = (holder_col == holder_row) & (
        iota((adapters, adapters), 1) < iota((adapters, adapters), 0)
    )
    rank_col = jnp.sum(jnp.where(earlier, 1.0, 0.0), axis=1, keepdims=True)
    uses = tokens_ref[...] == iota((adapters, rows), 0)
    owner_row = jnp.sum(jnp.where(uses, holder_col, 0.0), axis=0, keepdims=True)
    local_row = jnp.sum(jnp.where(uses, rank_col, 0.0), axis=0, keepdims=True)
    owner_col = to_column(owner_row)
    before = (owner_col == owner_row) & (iota((rows, rows), 0) < iota((rows, rows), 1))
    place_row = jnp.sum(jnp.where(before, 1.0, 0.0), axis=0, keepdims=True)
    owner_int = owner_row.astype(jnp.int32)
    if replicas & (replicas - 1) == 0:
        step_row = owner_int ^ me
    else:
        step_row = owner_int - me
        step_row = jnp.where(step_row < 0, step_row + replicas, step_row)
    target_row = step_row * block + place_row.astype(jnp.int32)
    target_col = to_column(target_row.astype(F32)).astype(jnp.int32)
    local_col = to_column(local_row)
    slots = replicas * block
    select = (target_row == iota((slots, rows), 0)).astype(F32).astype(BF16)
    restore = (target_col == iota((rows, slots), 1)).astype(F32)
    order_ref[...] = restore.astype(BF16)
    local_by_slot = jnp.sum(restore * local_col, axis=0, keepdims=True)
    for k in range(replicas):
        lane = k * block // LANES * LANES
        tail = jnp.broadcast_to(local_by_slot[:, lane : lane + LANES], (16, LANES))
        messages[k][width // LANES * block :, :] = tail.astype(BF16)
    for i, copy in enumerate(copies):
        copy.wait()
        moved = jnp.dot(
            select, x_buf[:, i * piece : (i + 1) * piece], preferred_element_type=F32
        ).astype(BF16)
        for k in range(replicas):
            for j in range(piece // LANES):
                at = (i * (piece // LANES) + j) * block
                messages[k][at : at + block, :] = moved[
                    k * block : (k + 1) * block, j * LANES : (j + 1) * LANES
                ]


def shrink_kernel(replicas, block, *refs):
    messages, down_ref, partial_ref, local_ref = refs[:replicas], *refs[replicas:]
    count, rank, width = down_ref.shape
    slots = replicas * block
    chunks = width // LANES
    gathered = [
        jnp.concatenate(
            [messages[k][j * block : (j + 1) * block, :] for j in range(chunks)], axis=1
        )
        for k in range(replicas)
    ]
    x_rows = jnp.concatenate(gathered, axis=0)
    parts = []
    for c in range(slots // LANES):
        lane_step = (iota((16, LANES), 1) + c * LANES) // block
        row = jnp.zeros((16, LANES), F32)
        for k in range(replicas):
            if k * block // LANES == c:
                row = jnp.where(
                    lane_step == k, messages[k][chunks * block :, :].astype(F32), row
                )
        parts.append(row)
    local = jnp.concatenate(parts, axis=1) if len(parts) > 1 else parts[0]
    local_ref[...] = local[:8]
    product = lax.dot_general(
        down_ref[...].reshape(count * rank, width),
        x_rows,
        (((1,), (1,)), ((), ())),
        preferred_element_type=F32,
    )
    total = jnp.zeros((rank, slots), F32)
    for a in range(count):
        total += jnp.where(local[:1] == a, product[a * rank : (a + 1) * rank], 0.0)
    partial_ref[...] = total


def expand_kernel(replicas, block, partial_ref, local_ref, up_ref, *returns):
    count, rank, columns = up_ref.shape
    shrink = jnp.sum(partial_ref[...], axis=0).astype(BF16).astype(F32)
    local = local_ref[:1]
    spread = jnp.concatenate(
        [jnp.where(local == a, shrink, 0.0) for a in range(count)], axis=0
    ).astype(BF16)
    term = lax.dot_general(
        spread,
        up_ref[...].reshape(count * rank, columns),
        (((0,), (0,)), ((), ())),
        preferred_element_type=F32,
    )
    term = (adapter_output_scale * term).astype(BF16)
    for k in range(replicas):
        returns[k][...] = term[k * block : (k + 1) * block]


def attention_kernel(
    kv_heads, refill_ref, q_ref, fresh_ref, key_ref, value_ref, part_ref, weight_ref, flat_ref
):
    tokens, heads, depth = q_ref.shape
    positions = key_ref.shape[1]
    group = heads // kv_heads
    scale = depth ** (-0.5)
    base = pl.program_id(0) * tokens
    q_flat = q_ref[...].reshape(tokens * heads, depth)
    cross = lax.dot_general(
        q_flat, fresh_ref[...], (((1,), (1,)), ((), ())), preferred_element_type=F32
    )
    shape = cross.shape
    own = iota(shape, 1) == (iota(shape, 0) // group)
    fresh = jnp.sum(jnp.where(own, cross, 0.0), axis=1, keepdims=True) * scale
    own_head = (iota((heads, positions), 1) % kv_heads) == (iota((heads, positions), 0) // group)
    eye = iota((heads, LANES), 1) == iota((heads, LANES), 0)
    for t in range(tokens):
        score = lax.dot_general(
            q_ref[t], key_ref[t], (((1,), (1,)), ((), ())), preferred_element_type=F32
        )
        keep = own_head & (refill_ref[base + t] != 1)
        score = jnp.where(keep, score * scale, mask_value)
        new = fresh[t * heads : (t + 1) * heads]
        top = jnp.maximum(jnp.max(score, axis=1, keepdims=True), new)
        weight = jnp.exp(score - top)
        new = jnp.exp(new - top)
        inverse = 1.0 / (jnp.sum(weight, axis=1, keepdims=True) + new)
        new = (new * inverse).astype(BF16).astype(F32)
        weight_ref[t : t + 1, :] = jnp.sum(jnp.where(eye, new, 0.0), axis=0, keepdims=True)
        flat_ref[t * heads : (t + 1) * heads, :] = jnp.dot(
            (weight * inverse).astype(BF16), value_ref[t], preferred_element_type=F32
        )
    for h in range(heads):
        part_ref[:, h * depth : (h + 1) * depth] = flat_ref[pl.ds(h, tokens, stride=heads), :]


def finish_kernel(replicas, kv_heads, heads, *refs):
    terms = refs[:replicas]
    order_ref, base_ref, part_ref, weight_ref, incoming_ref, attended_ref = refs[replicas:]
    depth = incoming_ref.shape[1] // kv_heads
    back = jnp.concatenate([term[...] for term in terms], axis=0)
    term = jnp.dot(order_ref[...], back, preferred_element_type=F32)
    incoming = (base_ref[...] + term).astype(BF16)
    incoming_ref[...] = incoming
    wide = incoming.astype(F32)
    for h in range(heads):
        k = h // (heads // kv_heads)
        at = slice(h * depth, (h + 1) * depth)
        attended_ref[:, at] = (
            part_ref[:, at] + weight_ref[:, h : h + 1] * wide[:, k * depth : (k + 1) * depth]
        ).astype(BF16)


def params(mib):
    return pltpu.CompilerParams(vmem_limit_bytes=mib * 2**20)


def cost(flops, size):
    return pl.CostEstimate(flops=flops, bytes_accessed=size, transcendentals=0)


def body(
    mesh_shape,
    normed_hidden_rows,
    queries,
    incoming_key,
    stored_key_cache,
    stored_value_cache,
    value_weight,
    adapter_down_weight,
    adapter_up_weight,
    token_adapter_index,
    adapter_holder_replica,
    refill,
):
    replicas = mesh_shape["replica"]
    rows, width = normed_hidden_rows.shape
    count, rank, slice_width = adapter_down_weight.shape
    columns = value_weight.shape[1]
    heads, depth = queries.shape[1:]
    kv_heads = incoming_key.shape[1]
    cache = stored_key_cache.shape[1]
    block = 16
    while block * replicas < rows:
        block *= 2
    slots = replicas * block
    message_rows = slice_width // LANES * block + 16
    pieces = 4

    routed = pl.pallas_call(
        functools.partial(route_kernel, replicas, block),
        out_shape=[jax.ShapeDtypeStruct((message_rows, LANES), BF16)] * replicas
        + [jax.ShapeDtypeStruct((rows, slots), BF16)],
        in_specs=[VMEM, VMEM, ANY],
        out_specs=[VMEM] * (replicas + 1),
        scratch_shapes=[
            pltpu.VMEM((rows, slice_width), BF16),
            pltpu.SemaphoreType.DMA((pieces,)),
        ],
        compiler_params=params(16),
        name="route",
    )(token_adapter_index.reshape(1, rows), adapter_holder_replica.reshape(1, -1), normed_hidden_rows)
    messages, order = routed[:replicas], routed[replicas]
    arrived = [messages[0]] + [None] * (replicas - 1)
    for k in range(replicas - 1, 0, -1):
        arrived[k] = lax.ppermute(messages[k], "replica", partner_pairs(replicas, k))

    tokens = 16
    part, new_weight = pl.pallas_call(
        functools.partial(attention_kernel, kv_heads),
        out_shape=[
            jax.ShapeDtypeStruct((rows, heads * depth), F32),
            jax.ShapeDtypeStruct((rows, LANES), F32),
        ],
        grid=(rows // tokens,),
        in_specs=[
            pl.BlockSpec(memory_space=pltpu.SMEM),
            pl.BlockSpec((tokens, heads, depth), lambda i: (i, 0, 0)),
            pl.BlockSpec((tokens * kv_heads, depth), lambda i: (i, 0)),
            pl.BlockSpec((tokens, cache * kv_heads, depth), lambda i: (i, 0, 0)),
            pl.BlockSpec((tokens, cache * kv_heads, depth), lambda i: (i, 0, 0)),
        ],
        out_specs=[
            pl.BlockSpec((tokens, heads * depth), lambda i: (i, 0)),
            pl.BlockSpec((tokens, LANES), lambda i: (i, 0)),
        ],
        scratch_shapes=[pltpu.VMEM((tokens * heads, depth), F32)],
        compiler_params=params(24),
        cost_estimate=cost(4 * rows * heads * cache * kv_heads * depth, 10 * 2**20),
        name="attend_cache",
    )(
        refill,
        queries,
        incoming_key.reshape(rows * kv_heads, depth),
        stored_key_cache.reshape(rows, cache * kv_heads, depth),
        stored_value_cache.reshape(rows, cache * kv_heads, depth),
    )
    base = jnp.dot(normed_hidden_rows, value_weight, preferred_element_type=F32)

    partial_shrink, local = pl.pallas_call(
        functools.partial(shrink_kernel, replicas, block),
        out_shape=[
            jax.ShapeDtypeStruct((rank, slots), F32),
            jax.ShapeDtypeStruct((8, slots), F32),
        ],
        in_specs=[VMEM] * (replicas + 1),
        out_specs=[VMEM] * 2,
        compiler_params=params(16),
        name="shrink",
    )(*arrived, adapter_down_weight)
    gathered = lax.all_gather(partial_shrink, "tensor", axis=0)
    returns = pl.pallas_call(
        functools.partial(expand_kernel, replicas, block),
        out_shape=[jax.ShapeDtypeStruct((block, columns), BF16)] * replicas,
        in_specs=[VMEM] * 3,
        out_specs=[VMEM] * replicas,
        compiler_params=params(16),
        name="expand",
    )(gathered, local, adapter_up_weight)
    terms = [returns[0]] + [
        lax.ppermute(returns[k], "replica", return_pairs(replicas, k)) for k in range(1, replicas)
    ]
    incoming_value, attended = pl.pallas_call(
        functools.partial(finish_kernel, replicas, kv_heads, heads),
        out_shape=[
            jax.ShapeDtypeStruct((rows, columns), BF16),
            jax.ShapeDtypeStruct((rows, heads * depth), BF16),
        ],
        in_specs=[VMEM] * (replicas + 4),
        out_specs=[VMEM] * 2,
        compiler_params=params(16),
        name="finish",
    )(*terms, order, base, part, new_weight)
    return (incoming_value, attended)


def solution(mesh):
    return jax.shard_map(
        functools.partial(body, dict(mesh.shape)),
        mesh=mesh,
        in_specs=(
            P(("groups", "replica"), None),
            P(("groups", "replica"), "tensor", None),
            P(("groups", "replica"), "tensor", None),
            P(("groups", "replica"), None, "tensor", None),
            P(("groups", "replica"), None, "tensor", None),
            P(None, "tensor"),
            P("replica", None, "tensor"),
            P("replica", None, "tensor"),
            P(("groups", "replica")),
            P("groups"),
            P(("groups", "replica")),
        ),
        out_specs=(P(("groups", "replica"), "tensor"), P(("groups", "replica"), "tensor")),
        check_vma=False,
    )
```

time: 110 us -> 79.5 us (0.72)
  Pallas kernels: 0 us -> 42.9 us
  waiting for transfers between devices: 44 us -> 10.6 us
  blocking collectives: 25.6 us -> 5.56 us
  between operations: 14.2 us -> 0.75 us
  matrix products: 15.7 us -> 2.98 us
  starting transfers between devices: 0.08 us -> 10.3 us
  other arithmetic: 4.68 us -> 0 us
    pallas_call x0 -> x5, Pallas kernels: none -> 42.9 us  [the longest x1 40 us: body(): pl.pallas_call(functools.partial(attention_kernel, kv_heads), out_shape=[...]
    all_gather x1 -> x0, waiting for transfers between devices: 33.5 us -> none  [body(): lax.all_gather(x_slice, 'replica', axis=0, tiled=True)]
    psum x1 -> x0, blocking collectives: 13 us -> none  [holder_shrink_output(): summed = lax.psum(partial_value, 'tensor')]
    dot_general x6 -> x1, matrix products: 15.7 us -> 2.98 us  [body(): base = jnp.dot(normed_hidden_rows, value_weight, preferred_element_type=F32)]
    ppermute x0 -> x6, waiting for transfers between devices: none -> 10.6 us  [the longest x3 10.6 us: body(): lax.ppermute(messages[k], 'replica', partner_pairs(replicas, k))]
    reduce_scatter x1 -> x0, waiting for transfers between devices: 10.5 us -> none  [body(): lax.psum_scatter(holder_expand_output(shrink_output, holder_mask, adapter...]
    ppermute x0 -> x6, starting transfers between devices: none -> 10.3 us  [the longest x3 5.68 us: body(): lax.ppermute(messages[k], 'replica', partner_pairs(replicas, k))]
    all_gather x1, blocking collectives: 12.6 us -> 5.56 us  [body(): gathered = lax.all_gather(partial_shrink, 'tensor', axis=0)]
  transfers between devices with their start and end apart: 2 -> 6, of which waited for: 2 -> 2; matrix products, arithmetic and copies ran while one was open for 11% -> 4% of each run, Pallas kernels for 0% -> 50%
where the time goes in v1:
time: 79.5 us; the launch traced here: 79.2 us
  Pallas kernels  42.9 us (54%)
  waiting for transfers between devices  10.6 us (13%)
  starting transfers between devices  10.3 us (13%)
  local copies, waits for them, and re-layouts  6.09 us (8%)
  blocking collectives  5.56 us (7%)
  matrix products  2.98 us (4%)
    pallas_call x1, Pallas kernels, body(): pl.pallas_call(functools.partial(attention_kernel, kv_heads), out_shape=[...  40 us
    ppermute x3, waiting for transfers between devices, body(): lax.ppermute(messages[k], 'replica', partner_pairs(replicas, k))  10.6 us
    unnamed x22, local copies, waits for them, and re-layouts  6.09 us
    ppermute x3, starting transfers between devices, body(): lax.ppermute(messages[k], 'replica', partner_pairs(replicas, k))  5.68 us
    all_gather x1, blocking collectives, body(): gathered = lax.all_gather(partial_shrink, 'tensor', axis=0)  5.56 us
    ppermute x3, starting transfers between devices, body(): lax.ppermute(returns[k], 'replica', return_pairs(replicas, k))  4.57 us
    dot_general x1, matrix products, body(): base = jnp.dot(normed_hidden_rows, value_weight, preferred_element_type=F32)  2.98 us
  transfers between devices with their start and end apart: 6, of which 2 were waited for; matrix products, arithmetic and copies ran while one was open for 4% of the time, Pallas kernels for 50%

profile of v1, /device:TPU:0, one launch (start us, length us, event | category | flops | bytes accessed | tf_op | source)
XLA Modules:
  0.0 79.2 jit_solution(15376004872476314919)
XLA Ops:
  0.6 1.6 %copy-done = bf16[128,8192]{1,0:T(8,128)(2,1)S(1)} copy-done((bf16[128,8192]{1,0:T(8,128)(2,1)S(1)}, bf16[128,8192]{1,0:T(8,128)(2,1)}, u32[]{:S(2)}) %copy-start) | copy-done | bytes 2097176
  2.2 0.7 copy-done.9
  2.9 0.7 copy-done.10
  3.5 1.1 %route.1 = (bf16[528,128]{1,0:T(8,128)(2,1)S(1)}, bf16[528,128]{1,0:T(8,128)(2,1)S(1)}, bf16[528,128]{1,0:T(8,128)(2,1)S(1)}, bf16[528,128]{1,0:T(8,128)(2,1)S(1)}, bf16[128,128]{1,0:T(8,128)(2,1)S(1)}) custom-call(s32[1,128]{1,0:T(1,128)S(1)} %bitcast.12, s32[1,16]{1,0:T(1,128)S(1)} %bitcast.13, bf16[128,8192]{1,0:T(8,128)(2,1)S(1)} %copy-done), custom_call_target="tpu_custom_call" | custom-call | tf_op jit(solution)/shard_map/route/pallas_call | solution.py:244
  4.7 3.1 %collective-permute-start = (bf16[528,128]{1,0:T(8,128)(2,1)S(1)}, bf16[528,128]{1,0:T(8,128)(2,1)S(1)}, u32[]{:S(2)}, u32[]{:S(2)}) collective-permute-start(bf16[528,128]{1,0:T(8,128)(2,1)S(1)} %get-tuple-element.16), channel_id=1, source_target_pairs={{0,4},{4,0},{8,12},{12,8},{1,5},{5,1},{9,13},{13,9},{2,6},{6,2},{1... | collective-permute-start | bytes 405512 | tf_op jit(solution)/shard_map/ppermute | solution.py:260
  7.8 2.6 %collective-permute-start.1 = (bf16[528,128]{1,0:T(8,128)(2,1)S(1)}, bf16[528,128]{1,0:T(8,128)(2,1)S(1)}, u32[]{:S(2)}, u32[]{:S(2)}) collective-permute-start(bf16[528,128]{1,0:T(8,128)(2,1)S(1)} %get-tuple-element.17), channel_id=1, source_target_pairs={{0,8},{4,12},{8,0},{12,4},{1,9},{5,13},{9,1},{13,5},{2,10},{6,14},... | collective-permute-start | bytes 405512 | tf_op jit(solution)/shard_map/ppermute | solution.py:260
  10.4 0.0 collective-permute-start.2
  10.4 2.6 %collective-permute-done.refs_1_ = bf16[528,128]{1,0:T(8,128)(2,1)S(1)} collective-permute-done((bf16[528,128]{1,0:T(8,128)(2,1)S(1)}, bf16[528,128]{1,0:T(8,128)(2,1)S(1)}, u32[]{:S(2)}, u32[]{:S(2)}) %collective-permute-start) | collective-permute-done | bytes 135200 | tf_op jit(solution)/shard_map/ppermute | solution.py:260
  13.0 8.0 %collective-permute-done.1.refs_2_ = bf16[528,128]{1,0:T(8,128)(2,1)S(1)} collective-permute-done((bf16[528,128]{1,0:T(8,128)(2,1)S(1)}, bf16[528,128]{1,0:T(8,128)(2,1)S(1)}, u32[]{:S(2)}, u32[]{:S(2)}) %collective-permute-start.1) | collective-permute-done | bytes 135200 | tf_op jit(solution)/shard_map/ppermute | solution.py:260
  21.0 0.0 collective-permute-done.2.refs_3_
  21.0 1.2 %copy-done.4 = bf16[4,64,2048]{2,1,0:T(8,128)(2,1)S(1)} copy-done((bf16[4,64,2048]{2,1,0:T(8,128)(2,1)S(1)}, bf16[4,64,2048]{2,1,0:T(8,128)(2,1)}, u32[]{:S(2)}) %copy-start.4) | copy-done | bytes 1048600
  22.2 0.4 shrink.1
  22.7 5.6 %all-gather = f32[256,128]{1,0:T(8,128)S(1)} all-gather(f32[64,128]{1,0:T(8,128)S(1)} %get-tuple-element.19), channel_id=2, replica_groups=mesh['groups'=2,'replica'=4,'tensor'=4] {'tensor'}, dimensions={0}, use_global_device_ids=true | all-gather | bytes 163840 | tf_op jit(solution)/shard_map/all_gather | solution.py:305
  28.2 0.9 %copy-done.6 = bf16[4,64,256]{2,1,0:T(8,128)(2,1)S(1)} copy-done((bf16[4,64,256]{2,1,0:T(8,128)(2,1)S(1)}, bf16[4,64,256]{2,1,0:T(8,128)(2,1)}, u32[]{:S(2)}) %copy-start.6) | copy-done | bytes 131096
  29.1 0.2 expand.1
  29.3 2.1 %collective-permute-start.3 = (bf16[32,256]{1,0:T(8,128)(2,1)S(1)}, bf16[32,256]{1,0:T(8,128)(2,1)S(1)}, u32[]{:S(2)}, u32[]{:S(2)}) collective-permute-start(bf16[32,256]{1,0:T(8,128)(2,1)S(1)} %get-tuple-element.22), channel_id=1, source_target_pairs={{4,0},{0,4},{12,8},{8,12},{5,1},{1,5},{13,9},{9,13},{6,2},{2,6},{1... | collective-permute-start | bytes 49160 | tf_op jit(solution)/shard_map/ppermute | solution.py:315
  31.4 1.1 %collective-permute-start.4 = (bf16[32,256]{1,0:T(8,128)(2,1)S(1)}, bf16[32,256]{1,0:T(8,128)(2,1)S(1)}, u32[]{:S(2)}, u32[]{:S(2)}) collective-permute-start(bf16[32,256]{1,0:T(8,128)(2,1)S(1)} %get-tuple-element.23), channel_id=1, source_target_pairs={{8,0},{12,4},{0,8},{4,12},{9,1},{13,5},{1,9},{5,13},{10,2},{14,6},... | collective-permute-start | bytes 49160 | tf_op jit(solution)/shard_map/ppermute | solution.py:315
  32.5 1.4 %collective-permute-start.5 = (bf16[32,256]{1,0:T(8,128)(2,1)S(1)}, bf16[32,256]{1,0:T(8,128)(2,1)S(1)}, u32[]{:S(2)}, u32[]{:S(2)}) collective-permute-start(bf16[32,256]{1,0:T(8,128)(2,1)S(1)} %get-tuple-element.24), channel_id=1, source_target_pairs={{12,0},{8,4},{4,8},{0,12},{13,1},{9,5},{5,9},{1,13},{14,2},{10,6},... | collective-permute-start | bytes 49160 | tf_op jit(solution)/shard_map/ppermute | solution.py:315
  33.9 3.0 %fusion.refs_5_ = f32[128,256]{1,0:T(8,128)S(1)} fusion(bf16[128,8192]{1,0:T(8,128)(2,1)S(1)} %copy-done.1, bf16[8192,256]{1,0:T(8,128)(2,1)} %param.16), kind=kOutput, calls=%fused_computation | convolution fusion | flops 536870912 | bytes 6422528 | tf_op jit(solution)/shard_map/dot_general | solution.py:292
  36.9 0.0 copy-start.5
  37.0 1.0 %copy-done.5 = bf16[128,16,128]{2,1,0:T(8,128)(2,1)S(1)} copy-done((bf16[128,16,128]{2,1,0:T(8,128)(2,1)S(1)}, bf16[128,16,128]{2,1,0:T(8,128)(2,1)}, u32[]{:S(2)}) %copy-start.5) | copy-done | bytes 524312
  38.0 40.0 %attend_cache.1 = (f32[128,2048]{1,0:T(8,128)S(1)}, f32[128,128]{1,0:T(8,128)S(1)}) custom-call(s32[128]{0:T(128)S(1)} %copy-done.8, bf16[128,16,128]{2,1,0:T(8,128)(2,1)S(1)} %copy-done.5, bf16[256,128]{1,0:T(8,128)(2,1)S(1)} %bitcast.11, bf16[128,128,128]{2,1,0:T(8,128)(2,1)S(1)} %bitcast.8, bf16[128,128,128]{2,1,0:T(8,128)(2,1)S(1)} %bitcast.9), custom_call_target="tpu_custom_call" | custom-call | flops 134217728 | bytes 10485760 | tf_op jit(solution)/shard_map/attend_cache/pallas_call | solution.py:263
  78.0 0.0 collective-permute-done.4.refs_2_
  78.0 1.2 %finish.1 = (bf16[128,256]{1,0:T(8,128)(2,1)}, bf16[128,2048]{1,0:T(8,128)(2,1)}) custom-call(bf16[32,256]{1,0:T(8,128)(2,1)S(1)} %get-tuple-element.21.refs_0_, bf16[32,256]{1,0:T(8,128)(2,1)S(1)} %collective-permute-done.3.refs_1_, bf16[32,256]{1,0:T(8,128)(2,1)S(1)} %collective-permute-done.4.refs_2_, bf16[32,256]{1,0:T(8,128)(2,1)S(1)} %collective-permute-done.5.refs_3_, ...), custom_call_target="tpu_custom_call" | custom-call | tf_op jit(solution)/shard_map/finish/pallas_call | solution.py:317
  (17 shorter events, 0.0 us)
Async XLA Ops:
  0.6 1.6 %copy-start = (bf16[128,8192]{1,0:T(8,128)(2,1)S(1)}, bf16[128,8192]{1,0:T(8,128)(2,1)}, u32[]{:S(2)}) copy-start(bf16[128,8192]{1,0:T(8,128)(2,1)} %x_ref.1) | copy-start | bytes 6291460
  2.2 0.7 copy-start.9
  2.9 0.7 copy-start.10
  3.5 30.4 %copy-start.1 = (bf16[128,8192]{1,0:T(8,128)(2,1)S(1)}, bf16[128,8192]{1,0:T(8,128)(2,1)}, u32[]{:S(2)}) copy-start(bf16[128,8192]{1,0:T(8,128)(2,1)} %x_ref.1) | copy-start | bytes 6291460
  4.7 8.3 %collective-permute-start = (bf16[528,128]{1,0:T(8,128)(2,1)S(1)}, bf16[528,128]{1,0:T(8,128)(2,1)S(1)}, u32[]{:S(2)}, u32[]{:S(2)}) collective-permute-start(bf16[528,128]{1,0:T(8,128)(2,1)S(1)} %get-tuple-element.16), channel_id=1, source_target_pairs={{0,4},{4,0},{8,12},{12,8},{1,5},{5,1},{9,13},{13,9},{2,6},{6,2},{1... | collective-permute-start | bytes 405512 | tf_op jit(solution)/shard_map/ppermute | solution.py:260
  7.8 13.2 %collective-permute-start.1 = (bf16[528,128]{1,0:T(8,128)(2,1)S(1)}, bf16[528,128]{1,0:T(8,128)(2,1)S(1)}, u32[]{:S(2)}, u32[]{:S(2)}) collective-permute-start(bf16[528,128]{1,0:T(8,128)(2,1)S(1)} %get-tuple-element.17), channel_id=1, source_target_pairs={{0,8},{4,12},{8,0},{12,4},{1,9},{5,13},{9,1},{13,5},{2,10},{6,14},... | collective-permute-start | bytes 405512 | tf_op jit(solution)/shard_map/ppermute | solution.py:260
  10.4 10.6 %collective-permute-start.2 = (bf16[528,128]{1,0:T(8,128)(2,1)S(1)}, bf16[528,128]{1,0:T(8,128)(2,1)S(1)}, u32[]{:S(2)}, u32[]{:S(2)}) collective-permute-start(bf16[528,128]{1,0:T(8,128)(2,1)S(1)} %get-tuple-element.18), channel_id=1, source_target_pairs={{0,12},{4,8},{8,4},{12,0},{1,13},{5,9},{9,5},{13,1},{2,14},{6,10},... | collective-permute-start | bytes 405512 | tf_op jit(solution)/shard_map/ppermute | solution.py:260
  21.0 15.9 %copy-start.8 = (s32[128]{0:T(128)S(1)}, s32[128]{0:T(128)}, u32[]{:S(2)}) copy-start(s32[128]{0:T(128)} %refill_ref.1) | copy-start | bytes 1540
  21.0 1.2 %copy-start.4 = (bf16[4,64,2048]{2,1,0:T(8,128)(2,1)S(1)}, bf16[4,64,2048]{2,1,0:T(8,128)(2,1)}, u32[]{:S(2)}) copy-start(bf16[4,64,2048]{2,1,0:T(8,128)(2,1)} %refs_4_.1) | copy-start | bytes 3145732
  22.2 14.7 %copy-start.2 = (bf16[128,64,2,128]{3,2,1,0:T(2,128)(2,1)S(1)}, bf16[128,64,2,128]{3,2,1,0:T(2,128)(2,1)}, u32[]{:S(2)}) copy-start(bf16[128,64,2,128]{3,2,1,0:T(2,128)(2,1)} %param.14) | copy-start | bytes 12582916
  22.2 14.7 %copy-start.3 = (bf16[128,64,2,128]{3,2,1,0:T(2,128)(2,1)S(1)}, bf16[128,64,2,128]{3,2,1,0:T(2,128)(2,1)}, u32[]{:S(2)}) copy-start(bf16[128,64,2,128]{3,2,1,0:T(2,128)(2,1)} %param.15) | copy-start | bytes 12582916
  28.2 0.9 %copy-start.6 = (bf16[4,64,256]{2,1,0:T(8,128)(2,1)S(1)}, bf16[4,64,256]{2,1,0:T(8,128)(2,1)}, u32[]{:S(2)}) copy-start(bf16[4,64,256]{2,1,0:T(8,128)(2,1)} %up_ref.1) | copy-start | bytes 393220
  29.1 7.8 %copy-start.7 = (bf16[128,2,128]{2,1,0:T(2,128)(2,1)S(1)}, bf16[128,2,128]{2,1,0:T(2,128)(2,1)}, u32[]{:S(2)}) copy-start(bf16[128,2,128]{2,1,0:T(2,128)(2,1)} %param.13) | copy-start | bytes 196612
  29.3 48.6 %collective-permute-start.3 = (bf16[32,256]{1,0:T(8,128)(2,1)S(1)}, bf16[32,256]{1,0:T(8,128)(2,1)S(1)}, u32[]{:S(2)}, u32[]{:S(2)}) collective-permute-start(bf16[32,256]{1,0:T(8,128)(2,1)S(1)} %get-tuple-element.22), channel_id=1, source_target_pairs={{4,0},{0,4},{12,8},{8,12},{5,1},{1,5},{13,9},{9,13},{6,2},{2,6},{1... | collective-permute-start | bytes 49160 | tf_op jit(solution)/shard_map/ppermute | solution.py:315
  31.4 46.5 %collective-permute-start.4 = (bf16[32,256]{1,0:T(8,128)(2,1)S(1)}, bf16[32,256]{1,0:T(8,128)(2,1)S(1)}, u32[]{:S(2)}, u32[]{:S(2)}) collective-permute-start(bf16[32,256]{1,0:T(8,128)(2,1)S(1)} %get-tuple-element.23), channel_id=1, source_target_pairs={{8,0},{12,4},{0,8},{4,12},{9,1},{13,5},{1,9},{5,13},{10,2},{14,6},... | collective-permute-start | bytes 49160 | tf_op jit(solution)/shard_map/ppermute | solution.py:315
  32.5 45.5 %collective-permute-start.5 = (bf16[32,256]{1,0:T(8,128)(2,1)S(1)}, bf16[32,256]{1,0:T(8,128)(2,1)S(1)}, u32[]{:S(2)}, u32[]{:S(2)}) collective-permute-start(bf16[32,256]{1,0:T(8,128)(2,1)S(1)} %get-tuple-element.24), channel_id=1, source_target_pairs={{12,0},{8,4},{4,8},{0,12},{13,1},{9,5},{5,9},{1,13},{14,2},{10,6},... | collective-permute-start | bytes 49160 | tf_op jit(solution)/shard_map/ppermute | solution.py:315
  36.9 1.0 %copy-start.5 = (bf16[128,16,128]{2,1,0:T(8,128)(2,1)S(1)}, bf16[128,16,128]{2,1,0:T(8,128)(2,1)}, u32[]{:S(2)}) copy-start(bf16[128,16,128]{2,1,0:T(8,128)(2,1)} %q_ref.1) | copy-start | bytes 1572868

commit v2 on v1

--- a/solution.py
+++ b/solution.py
@@ -11,7 +11,7 @@
 mask_value = -1e30
 LANES = 128
 VMEM = pl.BlockSpec(memory_space=pltpu.VMEM)
-ANY = pl.BlockSpec(memory_space=pl.ANY)
+HBM = pl.BlockSpec(memory_space=pltpu.HBM)
 F32 = jnp.float32
 BF16 = jnp.bfloat16
 
@@ -36,10 +36,17 @@
     return [(b, a) for a, b in partner_pairs(replicas, step)]
 
 
-def route_kernel(replicas, block, tokens_ref, holder_ref, x_ref, *refs):
-    messages, order_ref, x_buf, sems = refs[:replicas], refs[replicas], refs[-2], refs[-1]
+def route_kernel(replicas, block, tokens_hbm, holder_hbm, x_ref, *refs):
+    messages, order_ref = refs[:replicas], refs[replicas]
+    tokens_ref, holder_ref, x_buf, sems, small_sems = refs[replicas + 1 :]
     rows, width = x_buf.shape
     pieces = sems.shape[0]
+    small = [
+        pltpu.make_async_copy(tokens_hbm, tokens_ref, small_sems.at[0]),
+        pltpu.make_async_copy(holder_hbm, holder_ref, small_sems.at[1]),
+    ]
+    for copy in small:
+        copy.start()
     piece = width // pieces
     first = lax.axis_index("tensor") * width
     copies = [
@@ -52,6 +59,8 @@
     ]
     for copy in copies:
         copy.start()
+    for copy in small:
+        copy.wait()
     me = lax.axis_index("replica")
     adapters = holder_ref.shape[1]
     holder_row = holder_ref[...].astype(F32)
@@ -151,41 +160,109 @@
         returns[k][...] = term[k * block : (k + 1) * block]
 
 
-def attention_kernel(
-    kv_heads, refill_ref, q_ref, fresh_ref, key_ref, value_ref, part_ref, weight_ref, flat_ref
+def middle_kernel(
+    kv_heads,
+    refill_hbm,
+    fresh_hbm,
+    q_hbm,
+    key_hbm,
+    value_hbm,
+    x_hbm,
+    w_hbm,
+    part_ref,
+    weight_ref,
+    base_ref,
+    refill_ref,
+    fresh_ref,
+    q_ref,
+    key_ref,
+    value_ref,
+    x_ref,
+    w_ref,
+    flat_ref,
+    sems,
+    small_sems,
 ):
-    tokens, heads, depth = q_ref.shape
+    rows, heads, depth = q_ref.shape
     positions = key_ref.shape[1]
+    width = w_ref.shape[0]
+    pieces = sems.shape[0]
+    tokens = rows // pieces
+    piece = width // pieces
     group = heads // kv_heads
     scale = depth ** (-0.5)
-    base = pl.program_id(0) * tokens
-    q_flat = q_ref[...].reshape(tokens * heads, depth)
-    cross = lax.dot_general(
-        q_flat, fresh_ref[...], (((1,), (1,)), ((), ())), preferred_element_type=F32
-    )
-    shape = cross.shape
-    own = iota(shape, 1) == (iota(shape, 0) // group)
-    fresh = jnp.sum(jnp.where(own, cross, 0.0), axis=1, keepdims=True) * scale
-    own_head = (iota((heads, positions), 1) % kv_heads) == (iota((heads, positions), 0) // group)
-    eye = iota((heads, LANES), 1) == iota((heads, LANES), 0)
-    for t in range(tokens):
+    small = [
+        pltpu.make_async_copy(refill_hbm, refill_ref, small_sems.at[0]),
+        pltpu.make_async_copy(fresh_hbm, fresh_ref, small_sems.at[1]),
+    ]
+    for copy in small:
+        copy.start()
+    copies = []
+    for i in range(pieces):
+        some, columns = pl.ds(i * tokens, tokens), pl.ds(i * piece, piece)
+        copies.append(
+            [
+                pltpu.make_async_copy(q_hbm.at[some], q_ref.at[some], sems.at[i, 0]),
+                pltpu.make_async_copy(key_hbm.at[some], key_ref.at[some], sems.at[i, 1]),
+                pltpu.make_async_copy(value_hbm.at[some], value_ref.at[some], sems.at[i, 2]),
+                pltpu.make_async_copy(x_hbm.at[:, columns], x_ref.at[:, columns], sems.at[i, 3]),
+                pltpu.make_async_copy(w_hbm.at[columns], w_ref.at[columns], sems.at[i, 4]),
+            ]
+        )
+        for copy in copies[i]:
+            copy.start()
+    for copy in small:
+        copy.wait()
+    n = tokens * heads
+    own_fresh = iota((n, tokens * kv_heads), 1) == (iota((n, tokens * kv_heads), 0) // group)
+    own_head = (iota((n, positions), 1) % kv_heads) == ((iota((n, positions), 0) // group) % kv_heads)
+    eye = iota((n, LANES), 1) == (iota((n, LANES), 0) % heads)
+    refilled = refill_ref[...].astype(F32)
+    for i in range(pieces):
+        first = i * tokens
+        for copy in copies[i]:
+            copy.wait()
+        cross = lax.dot_general(
+            q_ref[first : first + tokens].reshape(n, depth),
+            fresh_ref[first * kv_heads : (first + tokens) * kv_heads, :],
+            (((1,), (1,)), ((), ())),
+            preferred_element_type=F32,
+        )
+        fresh = jnp.sum(jnp.where(own_fresh, cross, 0.0), axis=1, keepdims=True) * scale
+        mine = iota((n, rows), 1) == (first + iota((n, rows), 0) // heads)
+        blocked = jnp.sum(jnp.where(mine, refilled, 0.0), axis=1, keepdims=True)
         score = lax.dot_general(
-            q_ref[t], key_ref[t], (((1,), (1,)), ((), ())), preferred_element_type=F32
-        )
-        keep = own_head & (refill_ref[base + t] != 1)
+            q_ref[first : first + tokens],
+            key_ref[first : first + tokens],
+            (((2,), (2,)), ((0,), (0,))),
+            preferred_element_type=F32,
+        ).reshape(n, positions)
+        keep = own_head & (blocked != 1.0)
         score = jnp.where(keep, score * scale, mask_value)
-        new = fresh[t * heads : (t + 1) * heads]
-        top = jnp.maximum(jnp.max(score, axis=1, keepdims=True), new)
+        top = jnp.maximum(jnp.max(score, axis=1, keepdims=True), fresh)
         weight = jnp.exp(score - top)
-        new = jnp.exp(new - top)
+        new = jnp.exp(fresh - top)
         inverse = 1.0 / (jnp.sum(weight, axis=1, keepdims=True) + new)
         new = (new * inverse).astype(BF16).astype(F32)
-        weight_ref[t : t + 1, :] = jnp.sum(jnp.where(eye, new, 0.0), axis=0, keepdims=True)
-        flat_ref[t * heads : (t + 1) * heads, :] = jnp.dot(
-            (weight * inverse).astype(BF16), value_ref[t], preferred_element_type=F32
-        )
-    for h in range(heads):
-        part_ref[:, h * depth : (h + 1) * depth] = flat_ref[pl.ds(h, tokens, stride=heads), :]
+        weight_ref[first : first + tokens, :] = jnp.sum(
+            jnp.where(eye, new, 0.0).reshape(tokens, heads, LANES), axis=1
+        )
+        flat_ref[...] = lax.dot_general(
+            (weight * inverse).astype(BF16).reshape(tokens, heads, positions),
+            value_ref[first : first + tokens],
+            (((2,), (1,)), ((0,), (0,))),
+            preferred_element_type=F32,
+        ).reshape(n, depth)
+        for h in range(heads):
+            part_ref[first : first + tokens, h * depth : (h + 1) * depth] = flat_ref[
+                pl.ds(h, tokens, stride=heads), :
+            ]
+        product = jnp.dot(
+            x_ref[:, i * piece : (i + 1) * piece],
+            w_ref[i * piece : (i + 1) * piece, :],
+            preferred_element_type=F32,
+        )
+        base_ref[...] = product if i == 0 else base_ref[...] + product
 
 
 def finish_kernel(replicas, kv_heads, heads, *refs):
@@ -203,6 +280,10 @@
         attended_ref[:, at] = (
             part_ref[:, at] + weight_ref[:, h : h + 1] * wide[:, k * depth : (k + 1) * depth]
         ).astype(BF16)
+
+
+def in_hbm(*arrays):
+    return [pltpu.with_memory_space_constraint(array, pltpu.HBM) for array in arrays]
 
 
 def params(mib):
@@ -233,6 +314,7 @@
     columns = value_weight.shape[1]
     heads, depth = queries.shape[1:]
     kv_heads = incoming_key.shape[1]
+    adapters = adapter_holder_replica.shape[0]
     cache = stored_key_cache.shape[1]
     block = 16
     while block * replicas < rows:
@@ -245,51 +327,69 @@
         functools.partial(route_kernel, replicas, block),
         out_shape=[jax.ShapeDtypeStruct((message_rows, LANES), BF16)] * replicas
         + [jax.ShapeDtypeStruct((rows, slots), BF16)],
-        in_specs=[VMEM, VMEM, ANY],
+        in_specs=[HBM] * 3,
         out_specs=[VMEM] * (replicas + 1),
         scratch_shapes=[
+            pltpu.VMEM((1, rows), jnp.int32),
+            pltpu.VMEM((1, adapters), jnp.int32),
             pltpu.VMEM((rows, slice_width), BF16),
             pltpu.SemaphoreType.DMA((pieces,)),
+            pltpu.SemaphoreType.DMA((2,)),
         ],
         compiler_params=params(16),
         name="route",
-    )(token_adapter_index.reshape(1, rows), adapter_holder_replica.reshape(1, -1), normed_hidden_rows)
+    )(
+        *in_hbm(
+            token_adapter_index.reshape(1, rows),
+            adapter_holder_replica.reshape(1, adapters),
+            normed_hidden_rows,
+        )
+    )
     messages, order = routed[:replicas], routed[replicas]
     arrived = [messages[0]] + [None] * (replicas - 1)
     for k in range(replicas - 1, 0, -1):
         arrived[k] = lax.ppermute(messages[k], "replica", partner_pairs(replicas, k))
 
-    tokens = 16
-    part, new_weight = pl.pallas_call(
-        functools.partial(attention_kernel, kv_heads),
+    positions = cache * kv_heads
+    parts = max(1, rows // 32)
+    part, new_weight, base = pl.pallas_call(
+        functools.partial(middle_kernel, kv_heads),
         out_shape=[
             jax.ShapeDtypeStruct((rows, heads * depth), F32),
             jax.ShapeDtypeStruct((rows, LANES), F32),
+            jax.ShapeDtypeStruct((rows, columns), F32),
         ],
-        grid=(rows // tokens,),
-        in_specs=[
-            pl.BlockSpec(memory_space=pltpu.SMEM),
-            pl.BlockSpec((tokens, heads, depth), lambda i: (i, 0, 0)),
-            pl.BlockSpec((tokens * kv_heads, depth), lambda i: (i, 0)),
-            pl.BlockSpec((tokens, cache * kv_heads, depth), lambda i: (i, 0, 0)),
-            pl.BlockSpec((tokens, cache * kv_heads, depth), lambda i: (i, 0, 0)),
+        in_specs=[HBM] * 7,
+        out_specs=[VMEM] * 3,
+        scratch_shapes=[
+            pltpu.VMEM((1, rows), jnp.int32),
+            pltpu.VMEM((rows * kv_heads, depth), BF16),
+            pltpu.VMEM((rows, heads, depth), BF16),
+            pltpu.VMEM((rows, positions, depth), BF16),
+            pltpu.VMEM((rows, positions, depth), BF16),
+            pltpu.VMEM((rows, width), BF16),
+            pltpu.VMEM((width, columns), BF16),
+            pltpu.VMEM((rows // parts * heads, depth), F32),
+            pltpu.SemaphoreType.DMA((parts, 5)),
+            pltpu.SemaphoreType.DMA((2,)),
         ],
-        out_specs=[
-            pl.BlockSpec((tokens, heads * depth), lambda i: (i, 0)),
-            pl.BlockSpec((tokens, LANES), lambda i: (i, 0)),
-        ],
-        scratch_shapes=[pltpu.VMEM((tokens * heads, depth), F32)],
-        compiler_params=params(24),
-        cost_estimate=cost(4 * rows * heads * cache * kv_heads * depth, 10 * 2**20),
-        name="attend_cache",
+        compiler_params=params(32),
+        cost_estimate=cost(
+            4 * rows * heads * positions * depth + 2 * rows * width * columns, 15 * 2**20
+        ),
+        name="middle",
     )(
-        refill,
-        queries,
-        incoming_key.reshape(rows * kv_heads, depth),
-        stored_key_cache.reshape(rows, cache * kv_heads, depth),
-        stored_value_cache.reshape(rows, cache * kv_heads, depth),
-    )
-    base = jnp.dot(normed_hidden_rows, value_weight, preferred_element_type=F32)
+        *in_hbm(
+            refill.reshape(1, rows),
+            incoming_key.reshape(rows * kv_heads, depth),
+            queries,
+            stored_key_cache.reshape(rows, positions, depth),
+            stored_value_cache.reshape(rows, positions, depth),
+            normed_hidden_rows,
+            value_weight,
+        )
+    )
+    part, *arrived = lax.optimization_barrier((part, *arrived))
 
     partial_shrink, local = pl.pallas_call(
         functools.partial(shrink_kernel, replicas, block),

time: 79.5 us -> 36.9 us (0.46)
  Pallas kernels: 42.9 us -> 15 us
  local copies, waits for them, and re-layouts: 6.09 us -> 0.01 us
  waiting for transfers between devices: 10.6 us -> 5.54 us
  matrix products: 2.98 us -> 0 us
    pallas_call x1, Pallas kernels: 40 us -> 11.2 us  [body(): pl.pallas_call(functools.partial(middle_kernel, kv_heads), out_shape=[jax...]
    ppermute x3, waiting for transfers between devices: 10.6 us -> 0.01 us  [body(): lax.ppermute(messages[k], 'replica', partner_pairs(replicas, k))]
    unnamed x22 -> x4, local copies, waits for them, and re-layouts: 6.09 us -> 0.01 us
    ppermute x3, waiting for transfers between devices: 0.01 us -> 5.53 us  [body(): lax.ppermute(returns[k], 'replica', return_pairs(replicas, k))]
    dot_general x1 -> x0, matrix products: 2.98 us -> none  [body(): base = jnp.dot(normed_hidden_rows, value_weight, preferred_element_type=F32)]
    pallas_call x1, Pallas kernels: 1.12 us -> 1.93 us  [body(): pl.pallas_call(functools.partial(route_kernel, replicas, block), out_shap...]
  transfers between devices with their start and end apart: 6 -> 6, of which waited for: 2 -> 2; matrix products, arithmetic and copies ran while one was open for 4% -> 0% of each run, Pallas kernels for 50% -> 30%
where the time goes in v2:
time: 36.9 us; the launch traced here: 36.8 us
  Pallas kernels  15 us (41%)
  starting transfers between devices  10.1 us (27%)
  waiting for transfers between devices  5.54 us (15%)
  blocking collectives  5.43 us (15%)
  between operations  0.69 us (2%)
    pallas_call x1, Pallas kernels, body(): pl.pallas_call(functools.partial(middle_kernel, kv_heads), out_shape=[jax...  11.2 us
    ppermute x3, starting transfers between devices, body(): lax.ppermute(messages[k], 'replica', partner_pairs(replicas, k))  5.68 us
    ppermute x3, waiting for transfers between devices, body(): lax.ppermute(returns[k], 'replica', return_pairs(replicas, k))  5.53 us
    all_gather x1, blocking collectives, body(): gathered = lax.all_gather(partial_shrink, 'tensor', axis=0)  5.43 us
    ppermute x3, starting transfers between devices, body(): lax.ppermute(returns[k], 'replica', return_pairs(replicas, k))  4.45 us
    pallas_call x1, Pallas kernels, body(): pl.pallas_call(functools.partial(route_kernel, replicas, block), out_shap...  1.93 us
    pallas_call x1, Pallas kernels, body(): pl.pallas_call(functools.partial(finish_kernel, replicas, kv_heads, heads...  1.18 us
  transfers between devices with their start and end apart: 6, of which 2 were waited for; matrix products, arithmetic and copies ran while one was open for 0% of the time, Pallas kernels for 30%

profile of v2, /device:TPU:0, one launch (start us, length us, event | category | flops | bytes accessed | tf_op | source)
XLA Modules:
  0.0 36.8 jit_solution(3142686036548590579)
XLA Ops:
  0.6 1.9 %route.1 = (bf16[528,128]{1,0:T(8,128)(2,1)S(1)}, bf16[528,128]{1,0:T(8,128)(2,1)S(1)}, bf16[528,128]{1,0:T(8,128)(2,1)S(1)}, bf16[528,128]{1,0:T(8,128)(2,1)S(1)}, bf16[128,128]{1,0:T(8,128)(2,1)S(1)}) custom-call(s32[1,128]{1,0:T(1,128)} %bitcast.12, s32[1,16]{1,0:T(1,128)} %bitcast.13, bf16[128,8192]{1,0:T(8,128)(2,1)} %x_ref.1), custom_call_target="tpu_custom_call" | custom-call | tf_op jit(solution)/shard_map/route/pallas_call | solution.py:326
  2.6 3.1 %collective-permute-start = (bf16[528,128]{1,0:T(8,128)(2,1)S(1)}, bf16[528,128]{1,0:T(8,128)(2,1)S(1)}, u32[]{:S(2)}, u32[]{:S(2)}) collective-permute-start(bf16[528,128]{1,0:T(8,128)(2,1)S(1)} %get-tuple-element.23), channel_id=1, source_target_pairs={{0,4},{4,0},{8,12},{12,8},{1,5},{5,1},{9,13},{13,9},{2,6},{6,2},{1... | collective-permute-start | bytes 405512 | tf_op jit(solution)/shard_map/ppermute | solution.py:351
  5.7 2.6 %collective-permute-start.1 = (bf16[528,128]{1,0:T(8,128)(2,1)S(1)}, bf16[528,128]{1,0:T(8,128)(2,1)S(1)}, u32[]{:S(2)}, u32[]{:S(2)}) collective-permute-start(bf16[528,128]{1,0:T(8,128)(2,1)S(1)} %get-tuple-element.24), channel_id=1, source_target_pairs={{0,8},{4,12},{8,0},{12,4},{1,9},{5,13},{9,1},{13,5},{2,10},{6,14},... | collective-permute-start | bytes 405512 | tf_op jit(solution)/shard_map/ppermute | solution.py:351
  8.3 0.0 collective-permute-start.2
  8.3 0.0 copy-start
  8.3 0.0 copy-start.1
  8.3 11.2 %middle.1 = (f32[128,2048]{1,0:T(8,128)S(1)}, f32[128,128]{1,0:T(8,128)S(1)}, f32[128,256]{1,0:T(8,128)S(1)}) custom-call(s32[1,128]{1,0:T(1,128)} %bitcast.11, bf16[256,128]{1,0:T(8,128)(2,1)} %bitcast.10, bf16[128,16,128]{2,1,0:T(8,128)(2,1)} %q_hbm.1, bf16[128,128,128]{2,1,0:T(8,128)(2,1)} %bitcast.8, bf16[128,128,128]{2,1,0:T(8,128)(2,1)} %bitcast.9, ...), custom_call_target="tpu_custom_call" | custom-call | flops 671088640 | bytes 15728640 | tf_op jit(solution)/shard_map/middle/pallas_call | solution.py:355
  19.5 0.0 collective-permute-done.refs_1_
  19.5 0.0 collective-permute-done.1.refs_2_
  19.5 0.0 collective-permute-done.2.refs_3_
  19.5 0.0 copy-done
  19.5 0.5 %shrink.1 = (f32[64,128]{1,0:T(8,128)S(1)}, f32[8,128]{1,0:T(8,128)S(1)}) custom-call(bf16[528,128]{1,0:T(8,128)(2,1)S(1)} %get-tuple-element.26.refs_0_, bf16[528,128]{1,0:T(8,128)(2,1)S(1)} %collective-permute-done.refs_1_, bf16[528,128]{1,0:T(8,128)(2,1)S(1)} %collective-permute-done.1.refs_2_, bf16[528,128]{1,0:T(8,128)(2,1)S(1)} %collective-permute-done.2.refs_3_, ...), custom_call_target="tpu_custom_call" | custom-call | tf_op jit(solution)/shard_map/shrink/pallas_call | solution.py:394
  20.0 5.4 %all-gather = f32[256,128]{1,0:T(8,128)S(1)} all-gather(f32[64,128]{1,0:T(8,128)S(1)} %get-tuple-element.30), channel_id=2, replica_groups=mesh['groups'=2,'replica'=4,'tensor'=4] {'tensor'}, dimensions={0}, use_global_device_ids=true | all-gather | bytes 163840 | tf_op jit(solution)/shard_map/all_gather | solution.py:405
  25.4 0.0 copy-done.1
  25.4 0.2 expand.1
  25.6 1.5 %collective-permute-start.3 = (bf16[32,256]{1,0:T(8,128)(2,1)S(1)}, bf16[32,256]{1,0:T(8,128)(2,1)S(1)}, u32[]{:S(2)}, u32[]{:S(2)}) collective-permute-start(bf16[32,256]{1,0:T(8,128)(2,1)S(1)} %get-tuple-element.33), channel_id=1, source_target_pairs={{4,0},{0,4},{12,8},{8,12},{5,1},{1,5},{13,9},{9,13},{6,2},{2,6},{1... | collective-permute-start | bytes 49160 | tf_op jit(solution)/shard_map/ppermute | solution.py:415
  27.1 3.0 %collective-permute-start.4 = (bf16[32,256]{1,0:T(8,128)(2,1)S(1)}, bf16[32,256]{1,0:T(8,128)(2,1)S(1)}, u32[]{:S(2)}, u32[]{:S(2)}) collective-permute-start(bf16[32,256]{1,0:T(8,128)(2,1)S(1)} %get-tuple-element.34), channel_id=1, source_target_pairs={{8,0},{12,4},{0,8},{4,12},{9,1},{13,5},{1,9},{5,13},{10,2},{14,6},... | collective-permute-start | bytes 49160 | tf_op jit(solution)/shard_map/ppermute | solution.py:415
  30.1 0.0 collective-permute-start.5
  30.1 0.0 collective-permute-done.3.refs_1_
  30.1 1.9 %collective-permute-done.4.refs_2_ = bf16[32,256]{1,0:T(8,128)(2,1)S(1)} collective-permute-done((bf16[32,256]{1,0:T(8,128)(2,1)S(1)}, bf16[32,256]{1,0:T(8,128)(2,1)S(1)}, u32[]{:S(2)}, u32[]{:S(2)}) %collective-permute-start.4) | collective-permute-done | bytes 16416 | tf_op jit(solution)/shard_map/ppermute | solution.py:415
  32.0 3.6 %collective-permute-done.5.refs_3_ = bf16[32,256]{1,0:T(8,128)(2,1)S(1)} collective-permute-done((bf16[32,256]{1,0:T(8,128)(2,1)S(1)}, bf16[32,256]{1,0:T(8,128)(2,1)S(1)}, u32[]{:S(2)}, u32[]{:S(2)}) %collective-permute-start.5) | collective-permute-done | bytes 16416 | tf_op jit(solution)/shard_map/ppermute | solution.py:415
  35.6 1.2 %finish.1 = (bf16[128,256]{1,0:T(8,128)(2,1)}, bf16[128,2048]{1,0:T(8,128)(2,1)}) custom-call(bf16[32,256]{1,0:T(8,128)(2,1)S(1)} %get-tuple-element.32.refs_0_, bf16[32,256]{1,0:T(8,128)(2,1)S(1)} %collective-permute-done.3.refs_1_, bf16[32,256]{1,0:T(8,128)(2,1)S(1)} %collective-permute-done.4.refs_2_, bf16[32,256]{1,0:T(8,128)(2,1)S(1)} %collective-permute-done.5.refs_3_, ...), custom_call_target="tpu_custom_call" | custom-call | tf_op jit(solution)/shard_map/finish/pallas_call | solution.py:417
Async XLA Ops:
  2.6 16.9 %collective-permute-start = (bf16[528,128]{1,0:T(8,128)(2,1)S(1)}, bf16[528,128]{1,0:T(8,128)(2,1)S(1)}, u32[]{:S(2)}, u32[]{:S(2)}) collective-permute-start(bf16[528,128]{1,0:T(8,128)(2,1)S(1)} %get-tuple-element.23), channel_id=1, source_target_pairs={{0,4},{4,0},{8,12},{12,8},{1,5},{5,1},{9,13},{13,9},{2,6},{6,2},{1... | collective-permute-start | bytes 405512 | tf_op jit(solution)/shard_map/ppermute | solution.py:351
  5.7 13.8 %collective-permute-start.1 = (bf16[528,128]{1,0:T(8,128)(2,1)S(1)}, bf16[528,128]{1,0:T(8,128)(2,1)S(1)}, u32[]{:S(2)}, u32[]{:S(2)}) collective-permute-start(bf16[528,128]{1,0:T(8,128)(2,1)S(1)} %get-tuple-element.24), channel_id=1, source_target_pairs={{0,8},{4,12},{8,0},{12,4},{1,9},{5,13},{9,1},{13,5},{2,10},{6,14},... | collective-permute-start | bytes 405512 | tf_op jit(solution)/shard_map/ppermute | solution.py:351
  8.3 11.2 %collective-permute-start.2 = (bf16[528,128]{1,0:T(8,128)(2,1)S(1)}, bf16[528,128]{1,0:T(8,128)(2,1)S(1)}, u32[]{:S(2)}, u32[]{:S(2)}) collective-permute-start(bf16[528,128]{1,0:T(8,128)(2,1)S(1)} %get-tuple-element.25), channel_id=1, source_target_pairs={{0,12},{4,8},{8,4},{12,0},{1,13},{5,9},{9,5},{13,1},{2,14},{6,10},... | collective-permute-start | bytes 405512 | tf_op jit(solution)/shard_map/ppermute | solution.py:351
  8.3 11.3 %copy-start = (bf16[4,64,2048]{2,1,0:T(8,128)(2,1)S(1)}, bf16[4,64,2048]{2,1,0:T(8,128)(2,1)}, u32[]{:S(2)}) copy-start(bf16[4,64,2048]{2,1,0:T(8,128)(2,1)} %refs_4_.1) | copy-start | bytes 3145732
  8.3 17.1 %copy-start.1 = (bf16[4,64,256]{2,1,0:T(8,128)(2,1)S(1)}, bf16[4,64,256]{2,1,0:T(8,128)(2,1)}, u32[]{:S(2)}) copy-start(bf16[4,64,256]{2,1,0:T(8,128)(2,1)} %up_ref.1) | copy-start | bytes 393220
  25.6 4.5 %collective-permute-start.3 = (bf16[32,256]{1,0:T(8,128)(2,1)S(1)}, bf16[32,256]{1,0:T(8,128)(2,1)S(1)}, u32[]{:S(2)}, u32[]{:S(2)}) collective-permute-start(bf16[32,256]{1,0:T(8,128)(2,1)S(1)} %get-tuple-element.33), channel_id=1, source_target_pairs={{4,0},{0,4},{12,8},{8,12},{5,1},{1,5},{13,9},{9,13},{6,2},{2,6},{1... | collective-permute-start | bytes 49160 | tf_op jit(solution)/shard_map/ppermute | solution.py:415
  27.1 4.9 %collective-permute-start.4 = (bf16[32,256]{1,0:T(8,128)(2,1)S(1)}, bf16[32,256]{1,0:T(8,128)(2,1)S(1)}, u32[]{:S(2)}, u32[]{:S(2)}) collective-permute-start(bf16[32,256]{1,0:T(8,128)(2,1)S(1)} %get-tuple-element.34), channel_id=1, source_target_pairs={{8,0},{12,4},{0,8},{4,12},{9,1},{13,5},{1,9},{5,13},{10,2},{14,6},... | collective-permute-start | bytes 49160 | tf_op jit(solution)/shard_map/ppermute | solution.py:415
  30.1 5.5 %collective-permute-start.5 = (bf16[32,256]{1,0:T(8,128)(2,1)S(1)}, bf16[32,256]{1,0:T(8,128)(2,1)S(1)}, u32[]{:S(2)}, u32[]{:S(2)}) collective-permute-start(bf16[32,256]{1,0:T(8,128)(2,1)S(1)} %get-tuple-element.35), channel_id=1, source_target_pairs={{12,0},{8,4},{4,8},{0,12},{13,1},{9,5},{5,9},{1,13},{14,2},{10,6},... | collective-permute-start | bytes 49160 | tf_op jit(solution)/shard_map/ppermute | solution.py:415

commit v3 on v2

--- a/solution.py
+++ b/solution.py
@@ -9,6 +9,8 @@
 
 adapter_output_scale = 0.5
 mask_value = -1e30
+ahead = 2
+together = 2
 LANES = 128
 VMEM = pl.BlockSpec(memory_space=pltpu.VMEM)
 HBM = pl.BlockSpec(memory_space=pltpu.HBM)
@@ -106,8 +108,11 @@
                 ]
 
 
-def shrink_kernel(replicas, block, *refs):
-    messages, down_ref, partial_ref, local_ref = refs[:replicas], *refs[replicas:]
+def shrink_kernel(replicas, block, order_sent, *refs):
+    down_ref, partial_ref, local_ref = refs[replicas:]
+    messages = [None] * replicas
+    for k, ref in zip(order_sent, refs):
+        messages[k] = ref
     count, rank, width = down_ref.shape
     slots = replicas * block
     chunks = width // LANES
@@ -142,9 +147,14 @@
     partial_ref[...] = total
 
 
-def expand_kernel(replicas, block, partial_ref, local_ref, up_ref, *returns):
+def expand_kernel(shards, replicas, block, *refs):
+    partials, returns = refs[:shards], refs[shards + 2 :]
+    local_ref, up_ref = refs[shards : shards + 2]
     count, rank, columns = up_ref.shape
-    shrink = jnp.sum(partial_ref[...], axis=0).astype(BF16).astype(F32)
+    shrink = partials[0][...]
+    for partial in partials[1:]:
+        shrink += partial[...]
+    shrink = shrink.astype(BF16).astype(F32)
     local = local_ref[:1]
     spread = jnp.concatenate(
         [jnp.where(local == a, shrink, 0.0) for a in range(count)], axis=0
@@ -197,31 +207,50 @@
     ]
     for copy in small:
         copy.start()
-    copies = []
+    stages = []
     for i in range(pieces):
-        some, columns = pl.ds(i * tokens, tokens), pl.ds(i * piece, piece)
-        copies.append(
+        some = pl.ds(i * tokens, tokens)
+        stages.append(
             [
                 pltpu.make_async_copy(q_hbm.at[some], q_ref.at[some], sems.at[i, 0]),
                 pltpu.make_async_copy(key_hbm.at[some], key_ref.at[some], sems.at[i, 1]),
                 pltpu.make_async_copy(value_hbm.at[some], value_ref.at[some], sems.at[i, 2]),
-                pltpu.make_async_copy(x_hbm.at[:, columns], x_ref.at[:, columns], sems.at[i, 3]),
-                pltpu.make_async_copy(w_hbm.at[columns], w_ref.at[columns], sems.at[i, 4]),
             ]
         )
-        for copy in copies[i]:
+    for i in range(pieces):
+        some = pl.ds(i * piece, piece)
+        stages.append(
+            [
+                pltpu.make_async_copy(x_hbm.at[:, some], x_ref.at[:, some], sems.at[i, 3]),
+                pltpu.make_async_copy(w_hbm.at[some], w_ref.at[some], sems.at[i, 4]),
+            ]
+        )
+
+    def start(stage):
+        for copy in stages[stage] if stage < len(stages) else []:
             copy.start()
+
+    def wait(stage):
+        for copy in stages[stage]:
+            copy.wait()
+
+    for i in range(ahead):
+        start(i)
     for copy in small:
         copy.wait()
     n = tokens * heads
     own_fresh = iota((n, tokens * kv_heads), 1) == (iota((n, tokens * kv_heads), 0) // group)
-    own_head = (iota((n, positions), 1) % kv_heads) == ((iota((n, positions), 0) // group) % kv_heads)
+    wide = together * positions
+    row, lane = iota((n, wide), 0), iota((n, wide), 1)
+    own_head = (lane % kv_heads == row // group % kv_heads) & (
+        lane // positions == row // heads % together
+    )
     eye = iota((n, LANES), 1) == (iota((n, LANES), 0) % heads)
     refilled = refill_ref[...].astype(F32)
     for i in range(pieces):
         first = i * tokens
-        for copy in copies[i]:
-            copy.wait()
+        wait(i)
+        start(i + ahead)
         cross = lax.dot_general(
             q_ref[first : first + tokens].reshape(n, depth),
             fresh_ref[first * kv_heads : (first + tokens) * kv_heads, :],
@@ -232,11 +261,11 @@
         mine = iota((n, rows), 1) == (first + iota((n, rows), 0) // heads)
         blocked = jnp.sum(jnp.where(mine, refilled, 0.0), axis=1, keepdims=True)
         score = lax.dot_general(
-            q_ref[first : first + tokens],
-            key_ref[first : first + tokens],
+            q_ref[first : first + tokens].reshape(tokens // together, together * heads, depth),
+            key_ref[first : first + tokens].reshape(tokens // together, wide, depth),
             (((2,), (2,)), ((0,), (0,))),
             preferred_element_type=F32,
-        ).reshape(n, positions)
+        ).reshape(n, wide)
         keep = own_head & (blocked != 1.0)
         score = jnp.where(keep, score * scale, mask_value)
         top = jnp.maximum(jnp.max(score, axis=1, keepdims=True), fresh)
@@ -248,8 +277,8 @@
             jnp.where(eye, new, 0.0).reshape(tokens, heads, LANES), axis=1
         )
         flat_ref[...] = lax.dot_general(
-            (weight * inverse).astype(BF16).reshape(tokens, heads, positions),
-            value_ref[first : first + tokens],
+            (weight * inverse).astype(BF16).reshape(tokens // together, together * heads, wide),
+            value_ref[first : first + tokens].reshape(tokens // together, wide, depth),
             (((2,), (1,)), ((0,), (0,))),
             preferred_element_type=F32,
         ).reshape(n, depth)
@@ -257,6 +286,9 @@
             part_ref[first : first + tokens, h * depth : (h + 1) * depth] = flat_ref[
                 pl.ds(h, tokens, stride=heads), :
             ]
+    for i in range(pieces):
+        wait(pieces + i)
+        start(pieces + i + ahead)
         product = jnp.dot(
             x_ref[:, i * piece : (i + 1) * piece],
             w_ref[i * piece : (i + 1) * piece, :],
@@ -265,8 +297,10 @@
         base_ref[...] = product if i == 0 else base_ref[...] + product
 
 
-def finish_kernel(replicas, kv_heads, heads, *refs):
-    terms = refs[:replicas]
+def finish_kernel(replicas, kv_heads, heads, order_back, *refs):
+    terms = [None] * replicas
+    for k, ref in zip(order_back, refs):
+        terms[k] = ref
     order_ref, base_ref, part_ref, weight_ref, incoming_ref, attended_ref = refs[replicas:]
     depth = incoming_ref.shape[1] // kv_heads
     back = jnp.concatenate([term[...] for term in terms], axis=0)
@@ -347,11 +381,12 @@
     )
     messages, order = routed[:replicas], routed[replicas]
     arrived = [messages[0]] + [None] * (replicas - 1)
-    for k in range(replicas - 1, 0, -1):
+    order_sent = list(range(replicas - 1, 0, -1))
+    for k in order_sent:
         arrived[k] = lax.ppermute(messages[k], "replica", partner_pairs(replicas, k))
 
     positions = cache * kv_heads
-    parts = max(1, rows // 32)
+    parts = max(1, rows // 64)
     part, new_weight, base = pl.pallas_call(
         functools.partial(middle_kernel, kv_heads),
         out_shape=[
@@ -389,10 +424,12 @@
             value_weight,
         )
     )
-    part, *arrived = lax.optimization_barrier((part, *arrived))
+    part, *moved = lax.optimization_barrier((part, *[arrived[k] for k in order_sent]))
+    for k, message in zip(order_sent, moved):
+        arrived[k] = message
 
     partial_shrink, local = pl.pallas_call(
-        functools.partial(shrink_kernel, replicas, block),
+        functools.partial(shrink_kernel, replicas, block, order_sent + [0]),
         out_shape=[
             jax.ShapeDtypeStruct((rank, slots), F32),
             jax.ShapeDtypeStruct((8, slots), F32),
@@ -401,21 +438,25 @@
         out_specs=[VMEM] * 2,
         compiler_params=params(16),
         name="shrink",
-    )(*arrived, adapter_down_weight)
-    gathered = lax.all_gather(partial_shrink, "tensor", axis=0)
+    )(*[arrived[k] for k in order_sent + [0]], adapter_down_weight)
+    shards = mesh_shape["tensor"]
+    partials = [partial_shrink] + [
+        lax.ppermute(partial_shrink, "tensor", partner_pairs(shards, k)) for k in range(1, shards)
+    ]
     returns = pl.pallas_call(
-        functools.partial(expand_kernel, replicas, block),
+        functools.partial(expand_kernel, shards, replicas, block),
         out_shape=[jax.ShapeDtypeStruct((block, columns), BF16)] * replicas,
-        in_specs=[VMEM] * 3,
+        in_specs=[VMEM] * (shards + 2),
         out_specs=[VMEM] * replicas,
         compiler_params=params(16),
         name="expand",
-    )(gathered, local, adapter_up_weight)
+    )(*partials, local, adapter_up_weight)
     terms = [returns[0]] + [
         lax.ppermute(returns[k], "replica", return_pairs(replicas, k)) for k in range(1, replicas)
     ]
+    order_back = list(range(2, replicas)) + list(range(min(replicas, 2)))[::-1]
     incoming_value, attended = pl.pallas_call(
-        functools.partial(finish_kernel, replicas, kv_heads, heads),
+        functools.partial(finish_kernel, replicas, kv_heads, heads, order_back),
         out_shape=[
             jax.ShapeDtypeStruct((rows, columns), BF16),
             jax.ShapeDtypeStruct((rows, heads * depth), BF16),
@@ -424,7 +465,7 @@
         out_specs=[VMEM] * 2,
         compiler_params=params(16),
         name="finish",
-    )(*terms, order, base, part, new_weight)
+    )(*[terms[k] for k in order_back], order, base, part, new_weight)
     return (incoming_value, attended)
 
 

time: 36.9 us -> 31.6 us (0.86)
  blocking collectives: 5.43 us -> 0 us
  Pallas kernels: 15 us -> 11.4 us
  waiting for transfers between devices: 5.54 us -> 8.12 us
  starting transfers between devices: 10.1 us -> 11.2 us
    all_gather x1 -> x0, blocking collectives: 5.43 us -> none  [body(): gathered = lax.all_gather(partial_shrink, 'tensor', axis=0)]
    pallas_call x1, Pallas kernels: 11.2 us -> 7.63 us  [body(): pl.pallas_call(functools.partial(middle_kernel, kv_heads), out_shape=[jax...]
    ppermute x3, waiting for transfers between devices: 0.01 us -> 3.13 us  [body(): lax.ppermute(messages[k], 'replica', partner_pairs(replicas, k))]
    ppermute x3, waiting for transfers between devices: 5.53 us -> 2.69 us  [body(): lax.ppermute(returns[k], 'replica', return_pairs(replicas, k))]
    ppermute x0 -> x3, waiting for transfers between devices: none -> 2.3 us  [body(): lax.ppermute(partial_shrink, 'tensor', partner_pairs(shards, k))]
    ppermute x0 -> x3, starting transfers between devices: none -> 1.93 us  [body(): lax.ppermute(partial_shrink, 'tensor', partner_pairs(shards, k))]
    ppermute x3, starting transfers between devices: 4.45 us -> 3.55 us  [body(): lax.ppermute(returns[k], 'replica', return_pairs(replicas, k))]
  transfers between devices with their start and end apart: 6 -> 9, of which waited for: 2 -> 6; matrix products, arithmetic and copies ran while one was open for 0% -> 0% of each run, Pallas kernels for 30% -> 24%
where the time goes in v3:
time: 31.6 us; the launch traced here: 31.4 us
  Pallas kernels  11.4 us (36%)
  starting transfers between devices  11.2 us (35%)
  waiting for transfers between devices  8.12 us (26%)
  between operations  0.68 us (2%)
    pallas_call x1, Pallas kernels, body(): pl.pallas_call(functools.partial(middle_kernel, kv_heads), out_shape=[jax...  7.63 us
    ppermute x3, starting transfers between devices, body(): lax.ppermute(messages[k], 'replica', partner_pairs(replicas, k))  5.76 us
    ppermute x3, starting transfers between devices, body(): lax.ppermute(returns[k], 'replica', return_pairs(replicas, k))  3.55 us
    ppermute x3, waiting for transfers between devices, body(): lax.ppermute(messages[k], 'replica', partner_pairs(replicas, k))  3.13 us
    ppermute x3, waiting for transfers between devices, body(): lax.ppermute(returns[k], 'replica', return_pairs(replicas, k))  2.69 us
    ppermute x3, waiting for transfers between devices, body(): lax.ppermute(partial_shrink, 'tensor', partner_pairs(shards, k))  2.3 us
    pallas_call x1, Pallas kernels, body(): pl.pallas_call(functools.partial(route_kernel, replicas, block), out_shap...  1.93 us
    ppermute x3, starting transfers between devices, body(): lax.ppermute(partial_shrink, 'tensor', partner_pairs(shards, k))  1.93 us
  transfers between devices with their start and end apart: 9, of which 6 were waited for; matrix products, arithmetic and copies ran while one was open for 0% of the time, Pallas kernels for 24%

profile of v3, /device:TPU:0, one launch (start us, length us, event | category | flops | bytes accessed | tf_op | source)
XLA Modules:
  0.0 31.4 jit_solution(952297827072232501)
XLA Ops:
  0.6 1.9 %route.1 = (bf16[528,128]{1,0:T(8,128)(2,1)S(1)}, bf16[528,128]{1,0:T(8,128)(2,1)S(1)}, bf16[528,128]{1,0:T(8,128)(2,1)S(1)}, bf16[528,128]{1,0:T(8,128)(2,1)S(1)}, bf16[128,128]{1,0:T(8,128)(2,1)S(1)}) custom-call(s32[1,128]{1,0:T(1,128)} %bitcast.10, s32[1,16]{1,0:T(1,128)} %bitcast.11, bf16[128,8192]{1,0:T(8,128)(2,1)} %x_ref.1), custom_call_target="tpu_custom_call" | custom-call | tf_op jit(solution)/shard_map/route/pallas_call | solution.py:360
  2.6 5.1 %collective-permute-start = (bf16[528,128]{1,0:T(8,128)(2,1)S(1)}, bf16[528,128]{1,0:T(8,128)(2,1)S(1)}, u32[]{:S(2)}, u32[]{:S(2)}) collective-permute-start(bf16[528,128]{1,0:T(8,128)(2,1)S(1)} %get-tuple-element.21), channel_id=1, source_target_pairs={{0,12},{4,8},{8,4},{12,0},{1,13},{5,9},{9,5},{13,1},{2,14},{6,10},... | collective-permute-start | bytes 405512 | tf_op jit(solution)/shard_map/ppermute | solution.py:386
  7.7 0.0 collective-permute-start.1
  7.7 0.6 %collective-permute-start.2 = (bf16[528,128]{1,0:T(8,128)(2,1)S(1)}, bf16[528,128]{1,0:T(8,128)(2,1)S(1)}, u32[]{:S(2)}, u32[]{:S(2)}) collective-permute-start(bf16[528,128]{1,0:T(8,128)(2,1)S(1)} %get-tuple-element.23), channel_id=1, source_target_pairs={{0,4},{4,0},{8,12},{12,8},{1,5},{5,1},{9,13},{13,9},{2,6},{6,2},{1... | collective-permute-start | bytes 405512 | tf_op jit(solution)/shard_map/ppermute | solution.py:386
  8.3 7.6 %middle.1 = (f32[128,2048]{1,0:T(8,128)S(1)}, f32[128,128]{1,0:T(8,128)S(1)}, f32[128,256]{1,0:T(8,128)S(1)}) custom-call(s32[1,128]{1,0:T(1,128)} %bitcast.9, bf16[256,128]{1,0:T(8,128)(2,1)} %bitcast.8, bf16[128,16,128]{2,1,0:T(8,128)(2,1)} %q_hbm.1, bf16[128,128,128]{2,1,0:T(8,128)(2,1)} %bitcast.6, bf16[128,128,128]{2,1,0:T(8,128)(2,1)} %bitcast.7, ...), custom_call_target="tpu_custom_call" | custom-call | flops 671088640 | bytes 15728640 | tf_op jit(solution)/shard_map/middle/pallas_call | solution.py:390
  16.0 0.0 collective-permute-done.refs_0_
  16.0 3.1 %collective-permute-done.1.refs_1_ = bf16[528,128]{1,0:T(8,128)(2,1)S(1)} collective-permute-done((bf16[528,128]{1,0:T(8,128)(2,1)S(1)}, bf16[528,128]{1,0:T(8,128)(2,1)S(1)}, u32[]{:S(2)}, u32[]{:S(2)}) %collective-permute-start.1) | collective-permute-done | bytes 135200 | tf_op jit(solution)/shard_map/ppermute | solution.py:386
  19.1 0.0 collective-permute-done.2.refs_2_
  19.1 0.4 %shrink.1 = (f32[64,128]{1,0:T(8,128)S(1)}, f32[8,128]{1,0:T(8,128)S(1)}) custom-call(bf16[528,128]{1,0:T(8,128)(2,1)S(1)} %collective-permute-done.refs_0_, bf16[528,128]{1,0:T(8,128)(2,1)S(1)} %collective-permute-done.1.refs_1_, bf16[528,128]{1,0:T(8,128)(2,1)S(1)} %collective-permute-done.2.refs_2_, bf16[528,128]{1,0:T(8,128)(2,1)S(1)} %get-tuple-element.27.refs_3_, ...), custom_call_target="tpu_custom_call" | custom-call | tf_op jit(solution)/shard_map/shrink/pallas_call | solution.py:431
  19.6 0.3 collective-permute-start.5
  19.9 1.3 %collective-permute-start.4 = (f32[64,128]{1,0:T(8,128)S(1)}, f32[64,128]{1,0:T(8,128)S(1)}, u32[]{:S(2)}, u32[]{:S(2)}) collective-permute-start(f32[64,128]{1,0:T(8,128)S(1)} %get-tuple-element.28.refs_0_), channel_id=1, source_target_pairs={{0,2},{1,3},{2,0},{3,1},{4,6},{5,7},{6,4},{7,5},{8,10},{9,11},{10,... | collective-permute-start | bytes 98312 | tf_op jit(solution)/shard_map/ppermute | solution.py:444
  21.2 0.3 collective-permute-start.3
  21.5 1.8 %collective-permute-done.5.refs_3_ = f32[64,128]{1,0:T(8,128)S(1)} collective-permute-done((f32[64,128]{1,0:T(8,128)S(1)}, f32[64,128]{1,0:T(8,128)S(1)}, u32[]{:S(2)}, u32[]{:S(2)}) %collective-permute-start.5) | collective-permute-done | bytes 32800 | tf_op jit(solution)/shard_map/ppermute | solution.py:444
  23.3 0.5 %collective-permute-done.4.refs_2_ = f32[64,128]{1,0:T(8,128)S(1)} collective-permute-done((f32[64,128]{1,0:T(8,128)S(1)}, f32[64,128]{1,0:T(8,128)S(1)}, u32[]{:S(2)}, u32[]{:S(2)}) %collective-permute-start.4) | collective-permute-done | bytes 32800 | tf_op jit(solution)/shard_map/ppermute | solution.py:444
  23.8 0.0 collective-permute-done.3.refs_1_
  23.8 0.0 copy-done.1
  23.8 0.2 expand.1
  24.0 0.1 collective-permute-start.6
  24.1 2.4 %collective-permute-start.7 = (bf16[32,256]{1,0:T(8,128)(2,1)S(1)}, bf16[32,256]{1,0:T(8,128)(2,1)S(1)}, u32[]{:S(2)}, u32[]{:S(2)}) collective-permute-start(bf16[32,256]{1,0:T(8,128)(2,1)S(1)} %get-tuple-element.31), channel_id=1, source_target_pairs={{12,0},{8,4},{4,8},{0,12},{13,1},{9,5},{5,9},{1,13},{14,2},{10,6},... | collective-permute-start | bytes 49160 | tf_op jit(solution)/shard_map/ppermute | solution.py:455
  26.5 1.0 %collective-permute-start.8 = (bf16[32,256]{1,0:T(8,128)(2,1)S(1)}, bf16[32,256]{1,0:T(8,128)(2,1)S(1)}, u32[]{:S(2)}, u32[]{:S(2)}) collective-permute-start(bf16[32,256]{1,0:T(8,128)(2,1)S(1)} %get-tuple-element.32), channel_id=1, source_target_pairs={{4,0},{0,4},{12,8},{8,12},{5,1},{1,5},{13,9},{9,13},{6,2},{2,6},{1... | collective-permute-start | bytes 49160 | tf_op jit(solution)/shard_map/ppermute | solution.py:455
  27.6 1.1 %collective-permute-done.6.refs_0_ = bf16[32,256]{1,0:T(8,128)(2,1)S(1)} collective-permute-done((bf16[32,256]{1,0:T(8,128)(2,1)S(1)}, bf16[32,256]{1,0:T(8,128)(2,1)S(1)}, u32[]{:S(2)}, u32[]{:S(2)}) %collective-permute-start.6) | collective-permute-done | bytes 16416 | tf_op jit(solution)/shard_map/ppermute | solution.py:455
  28.7 1.0 %collective-permute-done.7.refs_1_ = bf16[32,256]{1,0:T(8,128)(2,1)S(1)} collective-permute-done((bf16[32,256]{1,0:T(8,128)(2,1)S(1)}, bf16[32,256]{1,0:T(8,128)(2,1)S(1)}, u32[]{:S(2)}, u32[]{:S(2)}) %collective-permute-start.7) | collective-permute-done | bytes 16416 | tf_op jit(solution)/shard_map/ppermute | solution.py:455
  29.7 0.6 %collective-permute-done.8.refs_2_ = bf16[32,256]{1,0:T(8,128)(2,1)S(1)} collective-permute-done((bf16[32,256]{1,0:T(8,128)(2,1)S(1)}, bf16[32,256]{1,0:T(8,128)(2,1)S(1)}, u32[]{:S(2)}, u32[]{:S(2)}) %collective-permute-start.8) | collective-permute-done | bytes 16416 | tf_op jit(solution)/shard_map/ppermute | solution.py:455
  30.3 1.2 %finish.1 = (bf16[128,256]{1,0:T(8,128)(2,1)}, bf16[128,2048]{1,0:T(8,128)(2,1)}) custom-call(bf16[32,256]{1,0:T(8,128)(2,1)S(1)} %collective-permute-done.6.refs_0_, bf16[32,256]{1,0:T(8,128)(2,1)S(1)} %collective-permute-done.7.refs_1_, bf16[32,256]{1,0:T(8,128)(2,1)S(1)} %collective-permute-done.8.refs_2_, bf16[32,256]{1,0:T(8,128)(2,1)S(1)} %get-tuple-element.33.refs_3_, ...), custom_call_target="tpu_custom_call" | custom-call | tf_op jit(solution)/shard_map/finish/pallas_call | solution.py:458
  (3 shorter events, 0.0 us)
Async XLA Ops:
  2.6 13.4 %collective-permute-start = (bf16[528,128]{1,0:T(8,128)(2,1)S(1)}, bf16[528,128]{1,0:T(8,128)(2,1)S(1)}, u32[]{:S(2)}, u32[]{:S(2)}) collective-permute-start(bf16[528,128]{1,0:T(8,128)(2,1)S(1)} %get-tuple-element.21), channel_id=1, source_target_pairs={{0,12},{4,8},{8,4},{12,0},{1,13},{5,9},{9,5},{13,1},{2,14},{6,10},... | collective-permute-start | bytes 405512 | tf_op jit(solution)/shard_map/ppermute | solution.py:386
  7.7 11.4 %collective-permute-start.1 = (bf16[528,128]{1,0:T(8,128)(2,1)S(1)}, bf16[528,128]{1,0:T(8,128)(2,1)S(1)}, u32[]{:S(2)}, u32[]{:S(2)}) collective-permute-start(bf16[528,128]{1,0:T(8,128)(2,1)S(1)} %get-tuple-element.22), channel_id=1, source_target_pairs={{0,8},{4,12},{8,0},{12,4},{1,9},{5,13},{9,1},{13,5},{2,10},{6,14},... | collective-permute-start | bytes 405512 | tf_op jit(solution)/shard_map/ppermute | solution.py:386
  7.7 11.4 %collective-permute-start.2 = (bf16[528,128]{1,0:T(8,128)(2,1)S(1)}, bf16[528,128]{1,0:T(8,128)(2,1)S(1)}, u32[]{:S(2)}, u32[]{:S(2)}) collective-permute-start(bf16[528,128]{1,0:T(8,128)(2,1)S(1)} %get-tuple-element.23), channel_id=1, source_target_pairs={{0,4},{4,0},{8,12},{12,8},{1,5},{5,1},{9,13},{13,9},{2,6},{6,2},{1... | collective-permute-start | bytes 405512 | tf_op jit(solution)/shard_map/ppermute | solution.py:386
  8.3 10.8 %copy-start = (bf16[4,64,2048]{2,1,0:T(8,128)(2,1)S(1)}, bf16[4,64,2048]{2,1,0:T(8,128)(2,1)}, u32[]{:S(2)}) copy-start(bf16[4,64,2048]{2,1,0:T(8,128)(2,1)} %refs_4_.1) | copy-start | bytes 3145732
  8.3 15.5 %copy-start.1 = (bf16[4,64,256]{2,1,0:T(8,128)(2,1)S(1)}, bf16[4,64,256]{2,1,0:T(8,128)(2,1)}, u32[]{:S(2)}) copy-start(bf16[4,64,256]{2,1,0:T(8,128)(2,1)} %refs_5_.1) | copy-start | bytes 393220
  19.6 3.7 %collective-permute-start.5 = (f32[64,128]{1,0:T(8,128)S(1)}, f32[64,128]{1,0:T(8,128)S(1)}, u32[]{:S(2)}, u32[]{:S(2)}) collective-permute-start(f32[64,128]{1,0:T(8,128)S(1)} %get-tuple-element.28.refs_0_), channel_id=1, source_target_pairs={{0,3},{1,2},{2,1},{3,0},{4,7},{5,6},{6,5},{7,4},{8,11},{9,10},{10,... | collective-permute-start | bytes 98312 | tf_op jit(solution)/shard_map/ppermute | solution.py:444
  19.9 3.9 %collective-permute-start.4 = (f32[64,128]{1,0:T(8,128)S(1)}, f32[64,128]{1,0:T(8,128)S(1)}, u32[]{:S(2)}, u32[]{:S(2)}) collective-permute-start(f32[64,128]{1,0:T(8,128)S(1)} %get-tuple-element.28.refs_0_), channel_id=1, source_target_pairs={{0,2},{1,3},{2,0},{3,1},{4,6},{5,7},{6,4},{7,5},{8,10},{9,11},{10,... | collective-permute-start | bytes 98312 | tf_op jit(solution)/shard_map/ppermute | solution.py:444
  21.2 2.6 %collective-permute-start.3 = (f32[64,128]{1,0:T(8,128)S(1)}, f32[64,128]{1,0:T(8,128)S(1)}, u32[]{:S(2)}, u32[]{:S(2)}) collective-permute-start(f32[64,128]{1,0:T(8,128)S(1)} %get-tuple-element.28.refs_0_), channel_id=1, source_target_pairs={{0,1},{1,0},{2,3},{3,2},{4,5},{5,4},{6,7},{7,6},{8,9},{9,8},{10,11... | collective-permute-start | bytes 98312 | tf_op jit(solution)/shard_map/ppermute | solution.py:444
  24.0 4.7 %collective-permute-start.6 = (bf16[32,256]{1,0:T(8,128)(2,1)S(1)}, bf16[32,256]{1,0:T(8,128)(2,1)S(1)}, u32[]{:S(2)}, u32[]{:S(2)}) collective-permute-start(bf16[32,256]{1,0:T(8,128)(2,1)S(1)} %get-tuple-element.30), channel_id=1, source_target_pairs={{8,0},{12,4},{0,8},{4,12},{9,1},{13,5},{1,9},{5,13},{10,2},{14,6},... | collective-permute-start | bytes 49160 | tf_op jit(solution)/shard_map/ppermute | solution.py:455
  24.1 5.6 %collective-permute-start.7 = (bf16[32,256]{1,0:T(8,128)(2,1)S(1)}, bf16[32,256]{1,0:T(8,128)(2,1)S(1)}, u32[]{:S(2)}, u32[]{:S(2)}) collective-permute-start(bf16[32,256]{1,0:T(8,128)(2,1)S(1)} %get-tuple-element.31), channel_id=1, source_target_pairs={{12,0},{8,4},{4,8},{0,12},{13,1},{9,5},{5,9},{1,13},{14,2},{10,6},... | collective-permute-start | bytes 49160 | tf_op jit(solution)/shard_map/ppermute | solution.py:455
  26.5 3.7 %collective-permute-start.8 = (bf16[32,256]{1,0:T(8,128)(2,1)S(1)}, bf16[32,256]{1,0:T(8,128)(2,1)S(1)}, u32[]{:S(2)}, u32[]{:S(2)}) collective-permute-start(bf16[32,256]{1,0:T(8,128)(2,1)S(1)} %get-tuple-element.32), channel_id=1, source_target_pairs={{4,0},{0,4},{12,8},{8,12},{5,1},{1,5},{13,9},{9,13},{6,2},{2,6},{1... | collective-permute-start | bytes 49160 | tf_op jit(solution)/shard_map/ppermute | solution.py:455

commit v4 on v3

--- a/solution.py
+++ b/solution.py
@@ -39,7 +39,7 @@
 
 
 def route_kernel(replicas, block, tokens_hbm, holder_hbm, x_ref, *refs):
-    messages, order_ref = refs[:replicas], refs[replicas]
+    messages, target_ref = refs[:replicas], refs[replicas]
     tokens_ref, holder_ref, x_buf, sems, small_sems = refs[replicas + 1 :]
     rows, width = x_buf.shape
     pieces = sems.shape[0]
@@ -72,29 +72,30 @@
     )
     rank_col = jnp.sum(jnp.where(earlier, 1.0, 0.0), axis=1, keepdims=True)
     uses = tokens_ref[...] == iota((adapters, rows), 0)
-    owner_row = jnp.sum(jnp.where(uses, holder_col, 0.0), axis=0, keepdims=True)
+    owner_row = jnp.sum(jnp.where(uses, holder_col, 0.0), axis=0, keepdims=True).astype(jnp.int32)
     local_row = jnp.sum(jnp.where(uses, rank_col, 0.0), axis=0, keepdims=True)
-    owner_col = to_column(owner_row)
-    before = (owner_col == owner_row) & (iota((rows, rows), 0) < iota((rows, rows), 1))
-    place_row = jnp.sum(jnp.where(before, 1.0, 0.0), axis=0, keepdims=True)
-    owner_int = owner_row.astype(jnp.int32)
+    owned = (owner_row == iota((max(replicas, 16), rows), 0)).astype(F32)
+    before = (iota((rows, rows), 0) < iota((rows, rows), 1)).astype(F32).astype(BF16)
+    count = jnp.dot(owned.astype(BF16), before, preferred_element_type=F32)
+    place_row = jnp.sum(owned * count, axis=0, keepdims=True).astype(jnp.int32)
     if replicas & (replicas - 1) == 0:
-        step_row = owner_int ^ me
+        step_row = owner_row ^ me
     else:
-        step_row = owner_int - me
+        step_row = owner_row - me
         step_row = jnp.where(step_row < 0, step_row + replicas, step_row)
-    target_row = step_row * block + place_row.astype(jnp.int32)
-    target_col = to_column(target_row.astype(F32)).astype(jnp.int32)
-    local_col = to_column(local_row)
+    target_row = step_row * block + place_row
+    target_ref[...] = target_row
     slots = replicas * block
     select = (target_row == iota((slots, rows), 0)).astype(F32).astype(BF16)
-    restore = (target_col == iota((rows, slots), 1)).astype(F32)
-    order_ref[...] = restore.astype(BF16)
-    local_by_slot = jnp.sum(restore * local_col, axis=0, keepdims=True)
+    local_by_slot = lax.dot_general(
+        jnp.broadcast_to(local_row, (16, rows)).astype(BF16),
+        select,
+        (((1,), (1,)), ((), ())),
+        preferred_element_type=F32,
+    ).astype(BF16)
     for k in range(replicas):
         lane = k * block // LANES * LANES
-        tail = jnp.broadcast_to(local_by_slot[:, lane : lane + LANES], (16, LANES))
-        messages[k][width // LANES * block :, :] = tail.astype(BF16)
+        messages[k][width // LANES * block :, :] = local_by_slot[:, lane : lane + LANES]
     for i, copy in enumerate(copies):
         copy.wait()
         moved = jnp.dot(
@@ -109,7 +110,7 @@
 
 
 def shrink_kernel(replicas, block, order_sent, *refs):
-    down_ref, partial_ref, local_ref = refs[replicas:]
+    down_ref, partial_ref, sent_ref, local_ref = refs[replicas:]
     messages = [None] * replicas
     for k, ref in zip(order_sent, refs):
         messages[k] = ref
@@ -145,6 +146,7 @@
     for a in range(count):
         total += jnp.where(local[:1] == a, product[a * rank : (a + 1) * rank], 0.0)
     partial_ref[...] = total
+    sent_ref[...] = total.astype(BF16)
 
 
 def expand_kernel(shards, replicas, block, *refs):
@@ -153,7 +155,7 @@
     count, rank, columns = up_ref.shape
     shrink = partials[0][...]
     for partial in partials[1:]:
-        shrink += partial[...]
+        shrink += partial[...].astype(F32)
     shrink = shrink.astype(BF16).astype(F32)
     local = local_ref[:1]
     spread = jnp.concatenate(
@@ -172,6 +174,7 @@
 
 def middle_kernel(
     kv_heads,
+    target_ref,
     refill_hbm,
     fresh_hbm,
     q_hbm,
@@ -182,6 +185,7 @@
     part_ref,
     weight_ref,
     base_ref,
+    order_ref,
     refill_ref,
     fresh_ref,
     q_ref,
@@ -238,6 +242,8 @@
         start(i)
     for copy in small:
         copy.wait()
+    target_col = to_column(target_ref[...].astype(F32)).astype(jnp.int32)
+    order_ref[...] = (target_col == iota(order_ref.shape, 1)).astype(F32).astype(BF16)
     n = tokens * heads
     own_fresh = iota((n, tokens * kv_heads), 1) == (iota((n, tokens * kv_heads), 0) // group)
     wide = together * positions
@@ -355,12 +361,12 @@
         block *= 2
     slots = replicas * block
     message_rows = slice_width // LANES * block + 16
-    pieces = 4
+    pieces = 1
 
     routed = pl.pallas_call(
         functools.partial(route_kernel, replicas, block),
         out_shape=[jax.ShapeDtypeStruct((message_rows, LANES), BF16)] * replicas
-        + [jax.ShapeDtypeStruct((rows, slots), BF16)],
+        + [jax.ShapeDtypeStruct((1, rows), jnp.int32)],
         in_specs=[HBM] * 3,
         out_specs=[VMEM] * (replicas + 1),
         scratch_shapes=[
@@ -379,7 +385,7 @@
             normed_hidden_rows,
         )
     )
-    messages, order = routed[:replicas], routed[replicas]
+    messages, target = routed[:replicas], routed[replicas]
     arrived = [messages[0]] + [None] * (replicas - 1)
     order_sent = list(range(replicas - 1, 0, -1))
     for k in order_sent:
@@ -387,15 +393,16 @@
 
     positions = cache * kv_heads
     parts = max(1, rows // 64)
-    part, new_weight, base = pl.pallas_call(
+    part, new_weight, base, order = pl.pallas_call(
         functools.partial(middle_kernel, kv_heads),
         out_shape=[
             jax.ShapeDtypeStruct((rows, heads * depth), F32),
             jax.ShapeDtypeStruct((rows, LANES), F32),
             jax.ShapeDtypeStruct((rows, columns), F32),
+            jax.ShapeDtypeStruct((rows, slots), BF16),
         ],
-        in_specs=[HBM] * 7,
-        out_specs=[VMEM] * 3,
+        in_specs=[VMEM] + [HBM] * 7,
+        out_specs=[VMEM] * 4,
         scratch_shapes=[
             pltpu.VMEM((1, rows), jnp.int32),
             pltpu.VMEM((rows * kv_heads, depth), BF16),
@@ -414,6 +421,7 @@
         ),
         name="middle",
     )(
+        target,
         *in_hbm(
             refill.reshape(1, rows),
             incoming_key.reshape(rows * kv_heads, depth),
@@ -428,20 +436,21 @@
     for k, message in zip(order_sent, moved):
         arrived[k] = message
 
-    partial_shrink, local = pl.pallas_call(
+    partial_shrink, sent_shrink, local = pl.pallas_call(
         functools.partial(shrink_kernel, replicas, block, order_sent + [0]),
         out_shape=[
             jax.ShapeDtypeStruct((rank, slots), F32),
+            jax.ShapeDtypeStruct((rank, slots), BF16),
             jax.ShapeDtypeStruct((8, slots), F32),
         ],
         in_specs=[VMEM] * (replicas + 1),
-        out_specs=[VMEM] * 2,
+        out_specs=[VMEM] * 3,
         compiler_params=params(16),
         name="shrink",
     )(*[arrived[k] for k in order_sent + [0]], adapter_down_weight)
     shards = mesh_shape["tensor"]
     partials = [partial_shrink] + [
-        lax.ppermute(partial_shrink, "tensor", partner_pairs(shards, k)) for k in range(1, shards)
+        lax.ppermute(sent_shrink, "tensor", partner_pairs(shards, k)) for k in range(1, shards)
     ]
     returns = pl.pallas_call(
         functools.partial(expand_kernel, shards, replicas, block),

time: 31.6 us -> 30.9 us (0.978)
  Pallas kernels: 11.4 us -> 10.9 us
    pallas_call x1, Pallas kernels: 1.93 us -> 1.4 us  [body(): pl.pallas_call(functools.partial(route_kernel, replicas, block), out_shap...]
  transfers between devices with their start and end apart: 9 -> 9, of which waited for: 6 -> 6; matrix products, arithmetic and copies ran while one was open for 0% -> 0% of each run, Pallas kernels for 24% -> 25%
where the time goes in v4:
time: 30.9 us; the launch traced here: 30.7 us
  starting transfers between devices  11.2 us (36%)
  Pallas kernels  10.9 us (35%)
  waiting for transfers between devices  7.87 us (25%)
  between operations  0.68 us (2%)
    pallas_call x1, Pallas kernels, body(): pl.pallas_call(functools.partial(middle_kernel, kv_heads), out_shape=[jax...  7.69 us
    ppermute x3, starting transfers between devices, body(): lax.ppermute(messages[k], 'replica', partner_pairs(replicas, k))  5.76 us
    ppermute x3, starting transfers between devices, body(): lax.ppermute(returns[k], 'replica', return_pairs(replicas, k))  3.55 us
    ppermute x3, waiting for transfers between devices, body(): lax.ppermute(messages[k], 'replica', partner_pairs(replicas, k))  3.08 us
    ppermute x3, waiting for transfers between devices, body(): lax.ppermute(returns[k], 'replica', return_pairs(replicas, k))  2.67 us
    ppermute x3, waiting for transfers between devices, body(): lax.ppermute(sent_shrink, 'tensor', partner_pairs(shards, k))  2.12 us
    ppermute x3, starting transfers between devices, body(): lax.ppermute(sent_shrink, 'tensor', partner_pairs(shards, k))  1.93 us
    pallas_call x1, Pallas kernels, body(): pl.pallas_call(functools.partial(route_kernel, replicas, block), out_shap...  1.4 us
  transfers between devices with their start and end apart: 9, of which 6 were waited for; matrix products, arithmetic and copies ran while one was open for 0% of the time, Pallas kernels for 25%

profile of v4, /device:TPU:0, one launch (start us, length us, event | category | flops | bytes accessed | tf_op | source)
XLA Modules:
  0.0 30.7 jit_solution(2468251160342789769)
XLA Ops:
  0.6 1.4 %route.1 = (bf16[528,128]{1,0:T(8,128)(2,1)S(1)}, bf16[528,128]{1,0:T(8,128)(2,1)S(1)}, bf16[528,128]{1,0:T(8,128)(2,1)S(1)}, bf16[528,128]{1,0:T(8,128)(2,1)S(1)}, s32[1,128]{1,0:T(1,128)S(1)}) custom-call(s32[1,128]{1,0:T(1,128)} %bitcast.10, s32[1,16]{1,0:T(1,128)} %bitcast.11, bf16[128,8192]{1,0:T(8,128)(2,1)} %x_hbm.1), custom_call_target="tpu_custom_call" | custom-call | tf_op jit(solution)/shard_map/route/pallas_call | solution.py:366
  2.0 5.1 %collective-permute-start = (bf16[528,128]{1,0:T(8,128)(2,1)S(1)}, bf16[528,128]{1,0:T(8,128)(2,1)S(1)}, u32[]{:S(2)}, u32[]{:S(2)}) collective-permute-start(bf16[528,128]{1,0:T(8,128)(2,1)S(1)} %get-tuple-element.24), channel_id=1, source_target_pairs={{0,12},{4,8},{8,4},{12,0},{1,13},{5,9},{9,5},{13,1},{2,14},{6,10},... | collective-permute-start | bytes 405512 | tf_op jit(solution)/shard_map/ppermute | solution.py:392
  7.1 0.0 collective-permute-start.1
  7.2 0.6 %collective-permute-start.2 = (bf16[528,128]{1,0:T(8,128)(2,1)S(1)}, bf16[528,128]{1,0:T(8,128)(2,1)S(1)}, u32[]{:S(2)}, u32[]{:S(2)}) collective-permute-start(bf16[528,128]{1,0:T(8,128)(2,1)S(1)} %get-tuple-element.26), channel_id=1, source_target_pairs={{0,4},{4,0},{8,12},{12,8},{1,5},{5,1},{9,13},{13,9},{2,6},{6,2},{1... | collective-permute-start | bytes 405512 | tf_op jit(solution)/shard_map/ppermute | solution.py:392
  7.8 7.7 %middle.1 = (f32[128,2048]{1,0:T(8,128)S(1)}, f32[128,128]{1,0:T(8,128)S(1)}, f32[128,256]{1,0:T(8,128)S(1)}, bf16[128,128]{1,0:T(8,128)(2,1)S(1)}) custom-call(s32[1,128]{1,0:T(1,128)S(1)} %get-tuple-element.22.target_ref, s32[1,128]{1,0:T(1,128)} %bitcast.9, bf16[256,128]{1,0:T(8,128)(2,1)} %bitcast.8, bf16[128,16,128]{2,1,0:T(8,128)(2,1)} %q_hbm.1, ...), custom_call_target="tpu_custom_call" | custom-call | flops 671088640 | bytes 15728640 | tf_op jit(solution)/shard_map/middle/pallas_call | solution.py:396
  15.5 0.0 collective-permute-done.refs_0_
  15.5 3.1 %collective-permute-done.1.refs_1_ = bf16[528,128]{1,0:T(8,128)(2,1)S(1)} collective-permute-done((bf16[528,128]{1,0:T(8,128)(2,1)S(1)}, bf16[528,128]{1,0:T(8,128)(2,1)S(1)}, u32[]{:S(2)}, u32[]{:S(2)}) %collective-permute-start.1) | collective-permute-done | bytes 135200 | tf_op jit(solution)/shard_map/ppermute | solution.py:392
  18.6 0.0 collective-permute-done.2.refs_2_
  18.6 0.0 copy-done
  18.6 0.4 %shrink.1 = (f32[64,128]{1,0:T(8,128)S(1)}, bf16[64,128]{1,0:T(8,128)(2,1)S(1)}, f32[8,128]{1,0:T(8,128)S(1)}) custom-call(bf16[528,128]{1,0:T(8,128)(2,1)S(1)} %collective-permute-done.refs_0_, bf16[528,128]{1,0:T(8,128)(2,1)S(1)} %collective-permute-done.1.refs_1_, bf16[528,128]{1,0:T(8,128)(2,1)S(1)} %collective-permute-done.2.refs_2_, ...), custom_call_target="tpu_custom_call" | custom-call | tf_op jit(solution)/shard_map/shrink/pallas_call | solution.py:439
  19.0 0.3 %collective-permute-start.5 = (bf16[64,128]{1,0:T(8,128)(2,1)S(1)}, bf16[64,128]{1,0:T(8,128)(2,1)S(1)}, u32[]{:S(2)}, u32[]{:S(2)}) collective-permute-start(bf16[64,128]{1,0:T(8,128)(2,1)S(1)} %get-tuple-element.32), channel_id=1, source_target_pairs={{0,3},{1,2},{2,1},{3,0},{4,7},{5,6},{6,5},{7,4},{8,11},{9,10},{10,... | collective-permute-start | bytes 49160 | tf_op jit(solution)/shard_map/ppermute | solution.py:453
  19.3 1.3 %collective-permute-start.4 = (bf16[64,128]{1,0:T(8,128)(2,1)S(1)}, bf16[64,128]{1,0:T(8,128)(2,1)S(1)}, u32[]{:S(2)}, u32[]{:S(2)}) collective-permute-start(bf16[64,128]{1,0:T(8,128)(2,1)S(1)} %get-tuple-element.32), channel_id=1, source_target_pairs={{0,2},{1,3},{2,0},{3,1},{4,6},{5,7},{6,4},{7,5},{8,10},{9,11},{10,... | collective-permute-start | bytes 49160 | tf_op jit(solution)/shard_map/ppermute | solution.py:453
  20.7 0.3 collective-permute-start.3
  21.0 1.4 %collective-permute-done.5.refs_3_ = bf16[64,128]{1,0:T(8,128)(2,1)S(1)} collective-permute-done((bf16[64,128]{1,0:T(8,128)(2,1)S(1)}, bf16[64,128]{1,0:T(8,128)(2,1)S(1)}, u32[]{:S(2)}, u32[]{:S(2)}) %collective-permute-start.5) | collective-permute-done | bytes 16416 | tf_op jit(solution)/shard_map/ppermute | solution.py:453
  22.4 0.7 %collective-permute-done.4.refs_2_ = bf16[64,128]{1,0:T(8,128)(2,1)S(1)} collective-permute-done((bf16[64,128]{1,0:T(8,128)(2,1)S(1)}, bf16[64,128]{1,0:T(8,128)(2,1)S(1)}, u32[]{:S(2)}, u32[]{:S(2)}) %collective-permute-start.4) | collective-permute-done | bytes 16416 | tf_op jit(solution)/shard_map/ppermute | solution.py:453
  23.1 0.0 collective-permute-done.3.refs_1_
  23.1 0.2 expand.1
  23.3 0.1 collective-permute-start.6
  23.4 2.4 %collective-permute-start.7 = (bf16[32,256]{1,0:T(8,128)(2,1)S(1)}, bf16[32,256]{1,0:T(8,128)(2,1)S(1)}, u32[]{:S(2)}, u32[]{:S(2)}) collective-permute-start(bf16[32,256]{1,0:T(8,128)(2,1)S(1)} %get-tuple-element.35), channel_id=1, source_target_pairs={{12,0},{8,4},{4,8},{0,12},{13,1},{9,5},{5,9},{1,13},{14,2},{10,6},... | collective-permute-start | bytes 49160 | tf_op jit(solution)/shard_map/ppermute | solution.py:464
  25.8 1.1 %collective-permute-start.8 = (bf16[32,256]{1,0:T(8,128)(2,1)S(1)}, bf16[32,256]{1,0:T(8,128)(2,1)S(1)}, u32[]{:S(2)}, u32[]{:S(2)}) collective-permute-start(bf16[32,256]{1,0:T(8,128)(2,1)S(1)} %get-tuple-element.36), channel_id=1, source_target_pairs={{4,0},{0,4},{12,8},{8,12},{5,1},{1,5},{13,9},{9,13},{6,2},{2,6},{1... | collective-permute-start | bytes 49160 | tf_op jit(solution)/shard_map/ppermute | solution.py:464
  26.9 1.1 %collective-permute-done.6.refs_0_ = bf16[32,256]{1,0:T(8,128)(2,1)S(1)} collective-permute-done((bf16[32,256]{1,0:T(8,128)(2,1)S(1)}, bf16[32,256]{1,0:T(8,128)(2,1)S(1)}, u32[]{:S(2)}, u32[]{:S(2)}) %collective-permute-start.6) | collective-permute-done | bytes 16416 | tf_op jit(solution)/shard_map/ppermute | solution.py:464
  28.0 1.0 %collective-permute-done.7.refs_1_ = bf16[32,256]{1,0:T(8,128)(2,1)S(1)} collective-permute-done((bf16[32,256]{1,0:T(8,128)(2,1)S(1)}, bf16[32,256]{1,0:T(8,128)(2,1)S(1)}, u32[]{:S(2)}, u32[]{:S(2)}) %collective-permute-start.7) | collective-permute-done | bytes 16416 | tf_op jit(solution)/shard_map/ppermute | solution.py:464
  29.0 0.5 %collective-permute-done.8.refs_2_ = bf16[32,256]{1,0:T(8,128)(2,1)S(1)} collective-permute-done((bf16[32,256]{1,0:T(8,128)(2,1)S(1)}, bf16[32,256]{1,0:T(8,128)(2,1)S(1)}, u32[]{:S(2)}, u32[]{:S(2)}) %collective-permute-start.8) | collective-permute-done | bytes 16416 | tf_op jit(solution)/shard_map/ppermute | solution.py:464
  29.5 1.2 %finish.1 = (bf16[128,256]{1,0:T(8,128)(2,1)}, bf16[128,2048]{1,0:T(8,128)(2,1)}) custom-call(bf16[32,256]{1,0:T(8,128)(2,1)S(1)} %collective-permute-done.6.refs_0_, bf16[32,256]{1,0:T(8,128)(2,1)S(1)} %collective-permute-done.7.refs_1_, bf16[32,256]{1,0:T(8,128)(2,1)S(1)} %collective-permute-done.8.refs_2_, bf16[32,256]{1,0:T(8,128)(2,1)S(1)} %get-tuple-element.37.refs_3_, ...), custom_call_target="tpu_custom_call" | custom-call | tf_op jit(solution)/shard_map/finish/pallas_call | solution.py:467
  (3 shorter events, 0.0 us)
Async XLA Ops:
  2.0 13.5 %collective-permute-start = (bf16[528,128]{1,0:T(8,128)(2,1)S(1)}, bf16[528,128]{1,0:T(8,128)(2,1)S(1)}, u32[]{:S(2)}, u32[]{:S(2)}) collective-permute-start(bf16[528,128]{1,0:T(8,128)(2,1)S(1)} %get-tuple-element.24), channel_id=1, source_target_pairs={{0,12},{4,8},{8,4},{12,0},{1,13},{5,9},{9,5},{13,1},{2,14},{6,10},... | collective-permute-start | bytes 405512 | tf_op jit(solution)/shard_map/ppermute | solution.py:392
  7.1 11.4 %collective-permute-start.1 = (bf16[528,128]{1,0:T(8,128)(2,1)S(1)}, bf16[528,128]{1,0:T(8,128)(2,1)S(1)}, u32[]{:S(2)}, u32[]{:S(2)}) collective-permute-start(bf16[528,128]{1,0:T(8,128)(2,1)S(1)} %get-tuple-element.25), channel_id=1, source_target_pairs={{0,8},{4,12},{8,0},{12,4},{1,9},{5,13},{9,1},{13,5},{2,10},{6,14},... | collective-permute-start | bytes 405512 | tf_op jit(solution)/shard_map/ppermute | solution.py:392
  7.2 11.4 %collective-permute-start.2 = (bf16[528,128]{1,0:T(8,128)(2,1)S(1)}, bf16[528,128]{1,0:T(8,128)(2,1)S(1)}, u32[]{:S(2)}, u32[]{:S(2)}) collective-permute-start(bf16[528,128]{1,0:T(8,128)(2,1)S(1)} %get-tuple-element.26), channel_id=1, source_target_pairs={{0,4},{4,0},{8,12},{12,8},{1,5},{5,1},{9,13},{13,9},{2,6},{6,2},{1... | collective-permute-start | bytes 405512 | tf_op jit(solution)/shard_map/ppermute | solution.py:392
  7.8 10.8 %copy-start = (bf16[4,64,2048]{2,1,0:T(8,128)(2,1)S(1)}, bf16[4,64,2048]{2,1,0:T(8,128)(2,1)}, u32[]{:S(2)}) copy-start(bf16[4,64,2048]{2,1,0:T(8,128)(2,1)} %refs_4_.1) | copy-start | bytes 3145732
  7.8 15.3 %copy-start.1 = (bf16[4,64,256]{2,1,0:T(8,128)(2,1)S(1)}, bf16[4,64,256]{2,1,0:T(8,128)(2,1)}, u32[]{:S(2)}) copy-start(bf16[4,64,256]{2,1,0:T(8,128)(2,1)} %refs_5_.1) | copy-start | bytes 393220
  19.0 3.4 %collective-permute-start.5 = (bf16[64,128]{1,0:T(8,128)(2,1)S(1)}, bf16[64,128]{1,0:T(8,128)(2,1)S(1)}, u32[]{:S(2)}, u32[]{:S(2)}) collective-permute-start(bf16[64,128]{1,0:T(8,128)(2,1)S(1)} %get-tuple-element.32), channel_id=1, source_target_pairs={{0,3},{1,2},{2,1},{3,0},{4,7},{5,6},{6,5},{7,4},{8,11},{9,10},{10,... | collective-permute-start | bytes 49160 | tf_op jit(solution)/shard_map/ppermute | solution.py:453
  19.3 3.7 %collective-permute-start.4 = (bf16[64,128]{1,0:T(8,128)(2,1)S(1)}, bf16[64,128]{1,0:T(8,128)(2,1)S(1)}, u32[]{:S(2)}, u32[]{:S(2)}) collective-permute-start(bf16[64,128]{1,0:T(8,128)(2,1)S(1)} %get-tuple-element.32), channel_id=1, source_target_pairs={{0,2},{1,3},{2,0},{3,1},{4,6},{5,7},{6,4},{7,5},{8,10},{9,11},{10,... | collective-permute-start | bytes 49160 | tf_op jit(solution)/shard_map/ppermute | solution.py:453
  20.7 2.4 %collective-permute-start.3 = (bf16[64,128]{1,0:T(8,128)(2,1)S(1)}, bf16[64,128]{1,0:T(8,128)(2,1)S(1)}, u32[]{:S(2)}, u32[]{:S(2)}) collective-permute-start(bf16[64,128]{1,0:T(8,128)(2,1)S(1)} %get-tuple-element.32), channel_id=1, source_target_pairs={{0,1},{1,0},{2,3},{3,2},{4,5},{5,4},{6,7},{7,6},{8,9},{9,8},{10,11... | collective-permute-start | bytes 49160 | tf_op jit(solution)/shard_map/ppermute | solution.py:453
  23.3 4.7 %collective-permute-start.6 = (bf16[32,256]{1,0:T(8,128)(2,1)S(1)}, bf16[32,256]{1,0:T(8,128)(2,1)S(1)}, u32[]{:S(2)}, u32[]{:S(2)}) collective-permute-start(bf16[32,256]{1,0:T(8,128)(2,1)S(1)} %get-tuple-element.34), channel_id=1, source_target_pairs={{8,0},{12,4},{0,8},{4,12},{9,1},{13,5},{1,9},{5,13},{10,2},{14,6},... | collective-permute-start | bytes 49160 | tf_op jit(solution)/shard_map/ppermute | solution.py:464
  23.4 5.6 %collective-permute-start.7 = (bf16[32,256]{1,0:T(8,128)(2,1)S(1)}, bf16[32,256]{1,0:T(8,128)(2,1)S(1)}, u32[]{:S(2)}, u32[]{:S(2)}) collective-permute-start(bf16[32,256]{1,0:T(8,128)(2,1)S(1)} %get-tuple-element.35), channel_id=1, source_target_pairs={{12,0},{8,4},{4,8},{0,12},{13,1},{9,5},{5,9},{1,13},{14,2},{10,6},... | collective-permute-start | bytes 49160 | tf_op jit(solution)/shard_map/ppermute | solution.py:464
  25.8 3.7 %collective-permute-start.8 = (bf16[32,256]{1,0:T(8,128)(2,1)S(1)}, bf16[32,256]{1,0:T(8,128)(2,1)S(1)}, u32[]{:S(2)}, u32[]{:S(2)}) collective-permute-start(bf16[32,256]{1,0:T(8,128)(2,1)S(1)} %get-tuple-element.36), channel_id=1, source_target_pairs={{4,0},{0,4},{12,8},{8,12},{5,1},{1,5},{13,9},{9,13},{6,2},{2,6},{1... | collective-permute-start | bytes 49160 | tf_op jit(solution)/shard_map/ppermute | solution.py:464

commit v5 on v4

--- a/solution.py
+++ b/solution.py
@@ -194,6 +194,7 @@
     x_ref,
     w_ref,
     flat_ref,
+    wide_ref,
     sems,
     small_sems,
 ):
@@ -251,7 +252,6 @@
     own_head = (lane % kv_heads == row // group % kv_heads) & (
         lane // positions == row // heads % together
     )
-    eye = iota((n, LANES), 1) == (iota((n, LANES), 0) % heads)
     refilled = refill_ref[...].astype(F32)
     for i in range(pieces):
         first = i * tokens
@@ -279,9 +279,7 @@
         new = jnp.exp(fresh - top)
         inverse = 1.0 / (jnp.sum(weight, axis=1, keepdims=True) + new)
         new = (new * inverse).astype(BF16).astype(F32)
-        weight_ref[first : first + tokens, :] = jnp.sum(
-            jnp.where(eye, new, 0.0).reshape(tokens, heads, LANES), axis=1
-        )
+        wide_ref[...] = jnp.broadcast_to(new, (n, depth))
         flat_ref[...] = lax.dot_general(
             (weight * inverse).astype(BF16).reshape(tokens // together, together * heads, wide),
             value_ref[first : first + tokens].reshape(tokens // together, wide, depth),
@@ -289,9 +287,9 @@
             preferred_element_type=F32,
         ).reshape(n, depth)
         for h in range(heads):
-            part_ref[first : first + tokens, h * depth : (h + 1) * depth] = flat_ref[
-                pl.ds(h, tokens, stride=heads), :
-            ]
+            at = slice(h * depth, (h + 1) * depth)
+            part_ref[first : first + tokens, at] = flat_ref[pl.ds(h, tokens, stride=heads), :]
+            weight_ref[first : first + tokens, at] = wide_ref[pl.ds(h, tokens, stride=heads), :]
     for i in range(pieces):
         wait(pieces + i)
         start(pieces + i + ahead)
@@ -307,19 +305,35 @@
     terms = [None] * replicas
     for k, ref in zip(order_back, refs):
         terms[k] = ref
-    order_ref, base_ref, part_ref, weight_ref, incoming_ref, attended_ref = refs[replicas:]
-    depth = incoming_ref.shape[1] // kv_heads
+    order_ref, base_ref, part_ref, weight_ref = refs[replicas : replicas + 4]
+    incoming_hbm, attended_hbm, incoming_ref, attended_ref, sems = refs[replicas + 4 :]
+    rows, columns = incoming_ref.shape
+    depth = columns // kv_heads
+    pieces = sems.shape[0]
+    piece = rows // pieces
     back = jnp.concatenate([term[...] for term in terms], axis=0)
-    term = jnp.dot(order_ref[...], back, preferred_element_type=F32)
-    incoming = (base_ref[...] + term).astype(BF16)
-    incoming_ref[...] = incoming
-    wide = incoming.astype(F32)
-    for h in range(heads):
-        k = h // (heads // kv_heads)
-        at = slice(h * depth, (h + 1) * depth)
-        attended_ref[:, at] = (
-            part_ref[:, at] + weight_ref[:, h : h + 1] * wide[:, k * depth : (k + 1) * depth]
-        ).astype(BF16)
+    copies = []
+    for i in range(pieces):
+        some = slice(i * piece, (i + 1) * piece)
+        term = jnp.dot(order_ref[some, :], back, preferred_element_type=F32)
+        incoming = (base_ref[some, :] + term).astype(BF16)
+        incoming_ref[some, :] = incoming
+        wide = incoming.astype(F32)
+        for h in range(heads):
+            k = h // (heads // kv_heads)
+            at = slice(h * depth, (h + 1) * depth)
+            attended_ref[some, at] = (
+                part_ref[some, at] + weight_ref[some, at] * wide[:, k * depth : (k + 1) * depth]
+            ).astype(BF16)
+        lines = pl.ds(i * piece, piece)
+        for j, (source, result) in enumerate(
+            [(incoming_ref, incoming_hbm), (attended_ref, attended_hbm)]
+        ):
+            copy = pltpu.make_async_copy(source.at[lines], result.at[lines], sems.at[i, j])
+            copy.start()
+            copies.append(copy)
+    for copy in copies:
+        copy.wait()
 
 
 def in_hbm(*arrays):
@@ -397,7 +411,7 @@
         functools.partial(middle_kernel, kv_heads),
         out_shape=[
             jax.ShapeDtypeStruct((rows, heads * depth), F32),
-            jax.ShapeDtypeStruct((rows, LANES), F32),
+            jax.ShapeDtypeStruct((rows, heads * depth), F32),
             jax.ShapeDtypeStruct((rows, columns), F32),
             jax.ShapeDtypeStruct((rows, slots), BF16),
         ],
@@ -411,6 +425,7 @@
             pltpu.VMEM((rows, positions, depth), BF16),
             pltpu.VMEM((rows, width), BF16),
             pltpu.VMEM((width, columns), BF16),
+            pltpu.VMEM((rows // parts * heads, depth), F32),
             pltpu.VMEM((rows // parts * heads, depth), F32),
             pltpu.SemaphoreType.DMA((parts, 5)),
             pltpu.SemaphoreType.DMA((2,)),
@@ -463,6 +478,7 @@
     terms = [returns[0]] + [
         lax.ppermute(returns[k], "replica", return_pairs(replicas, k)) for k in range(1, replicas)
     ]
+    out_pieces = 4
     order_back = list(range(2, replicas)) + list(range(min(replicas, 2)))[::-1]
     incoming_value, attended = pl.pallas_call(
         functools.partial(finish_kernel, replicas, kv_heads, heads, order_back),
@@ -471,7 +487,12 @@
             jax.ShapeDtypeStruct((rows, heads * depth), BF16),
         ],
         in_specs=[VMEM] * (replicas + 4),
-        out_specs=[VMEM] * 2,
+        out_specs=[HBM] * 2,
+        scratch_shapes=[
+            pltpu.VMEM((rows, columns), BF16),
+            pltpu.VMEM((rows, heads * depth), BF16),
+            pltpu.SemaphoreType.DMA((out_pieces, 2)),
+        ],
         compiler_params=params(16),
         name="finish",
     )(*[terms[k] for k in order_back], order, base, part, new_weight)

time: 30.9 us -> 30.7 us (level)
  no operation moved by 1% of the time
where the time goes in v5:
time: 30.7 us; the launch traced here: 30.6 us
  starting transfers between devices  11.2 us (36%)
  Pallas kernels  10.8 us (35%)
  waiting for transfers between devices  7.91 us (26%)
  between operations  0.68 us (2%)
    pallas_call x1, Pallas kernels, body(): pl.pallas_call(functools.partial(middle_kernel, kv_heads), out_shape=[jax...  7.64 us
    ppermute x3, starting transfers between devices, body(): lax.ppermute(messages[k], 'replica', partner_pairs(replicas, k))  5.76 us
    ppermute x3, starting transfers between devices, body(): lax.ppermute(returns[k], 'replica', return_pairs(replicas, k))  3.55 us
    ppermute x3, waiting for transfers between devices, body(): lax.ppermute(messages[k], 'replica', partner_pairs(replicas, k))  3.12 us
    ppermute x3, waiting for transfers between devices, body(): lax.ppermute(returns[k], 'replica', return_pairs(replicas, k))  2.67 us
    ppermute x3, waiting for transfers between devices, body(): lax.ppermute(sent_shrink, 'tensor', partner_pairs(shards, k))  2.12 us
    ppermute x3, starting transfers between devices, body(): lax.ppermute(sent_shrink, 'tensor', partner_pairs(shards, k))  1.93 us
    pallas_call x1, Pallas kernels, body(): pl.pallas_call(functools.partial(route_kernel, replicas, block), out_shap...  1.4 us
  transfers between devices with their start and end apart: 9, of which 6 were waited for; matrix products, arithmetic and copies ran while one was open for 0% of the time, Pallas kernels for 25%

profile of v5, /device:TPU:0, one launch (start us, length us, event | category | flops | bytes accessed | tf_op | source)
XLA Modules:
  0.0 30.6 jit_solution(6604458600394627897)
XLA Ops:
  0.6 1.4 %route.1 = (bf16[528,128]{1,0:T(8,128)(2,1)S(1)}, bf16[528,128]{1,0:T(8,128)(2,1)S(1)}, bf16[528,128]{1,0:T(8,128)(2,1)S(1)}, bf16[528,128]{1,0:T(8,128)(2,1)S(1)}, s32[1,128]{1,0:T(1,128)S(1)}) custom-call(s32[1,128]{1,0:T(1,128)} %bitcast.10, s32[1,16]{1,0:T(1,128)} %bitcast.11, bf16[128,8192]{1,0:T(8,128)(2,1)} %x_hbm.1), custom_call_target="tpu_custom_call" | custom-call | tf_op jit(solution)/shard_map/route/pallas_call | solution.py:380
  2.0 5.1 %collective-permute-start = (bf16[528,128]{1,0:T(8,128)(2,1)S(1)}, bf16[528,128]{1,0:T(8,128)(2,1)S(1)}, u32[]{:S(2)}, u32[]{:S(2)}) collective-permute-start(bf16[528,128]{1,0:T(8,128)(2,1)S(1)} %get-tuple-element.24), channel_id=1, source_target_pairs={{0,12},{4,8},{8,4},{12,0},{1,13},{5,9},{9,5},{13,1},{2,14},{6,10},... | collective-permute-start | bytes 405512 | tf_op jit(solution)/shard_map/ppermute | solution.py:406
  7.1 0.0 collective-permute-start.1
  7.2 0.6 %collective-permute-start.2 = (bf16[528,128]{1,0:T(8,128)(2,1)S(1)}, bf16[528,128]{1,0:T(8,128)(2,1)S(1)}, u32[]{:S(2)}, u32[]{:S(2)}) collective-permute-start(bf16[528,128]{1,0:T(8,128)(2,1)S(1)} %get-tuple-element.26), channel_id=1, source_target_pairs={{0,4},{4,0},{8,12},{12,8},{1,5},{5,1},{9,13},{13,9},{2,6},{6,2},{1... | collective-permute-start | bytes 405512 | tf_op jit(solution)/shard_map/ppermute | solution.py:406
  7.8 7.6 %middle.1 = (f32[128,2048]{1,0:T(8,128)S(1)}, f32[128,2048]{1,0:T(8,128)S(1)}, f32[128,256]{1,0:T(8,128)S(1)}, bf16[128,128]{1,0:T(8,128)(2,1)S(1)}) custom-call(s32[1,128]{1,0:T(1,128)S(1)} %get-tuple-element.22.target_ref, s32[1,128]{1,0:T(1,128)} %bitcast.9, bf16[256,128]{1,0:T(8,128)(2,1)} %bitcast.8, bf16[128,16,128]{2,1,0:T(8,128)(2,1)} %q_hbm.1, ...), custom_call_target="tpu_custom_call" | custom-call | flops 671088640 | bytes 15728640 | tf_op jit(solution)/shard_map/middle/pallas_call | solution.py:410
  15.4 0.0 collective-permute-done.refs_0_
  15.5 3.1 %collective-permute-done.1.refs_1_ = bf16[528,128]{1,0:T(8,128)(2,1)S(1)} collective-permute-done((bf16[528,128]{1,0:T(8,128)(2,1)S(1)}, bf16[528,128]{1,0:T(8,128)(2,1)S(1)}, u32[]{:S(2)}, u32[]{:S(2)}) %collective-permute-start.1) | collective-permute-done | bytes 135200 | tf_op jit(solution)/shard_map/ppermute | solution.py:406
  18.6 0.0 collective-permute-done.2.refs_2_
  18.6 0.4 %shrink.1 = (f32[64,128]{1,0:T(8,128)S(1)}, bf16[64,128]{1,0:T(8,128)(2,1)S(1)}, f32[8,128]{1,0:T(8,128)S(1)}) custom-call(bf16[528,128]{1,0:T(8,128)(2,1)S(1)} %collective-permute-done.refs_0_, bf16[528,128]{1,0:T(8,128)(2,1)S(1)} %collective-permute-done.1.refs_1_, bf16[528,128]{1,0:T(8,128)(2,1)S(1)} %collective-permute-done.2.refs_2_, ...), custom_call_target="tpu_custom_call" | custom-call | tf_op jit(solution)/shard_map/shrink/pallas_call | solution.py:454
  19.0 0.3 %collective-permute-start.5 = (bf16[64,128]{1,0:T(8,128)(2,1)S(1)}, bf16[64,128]{1,0:T(8,128)(2,1)S(1)}, u32[]{:S(2)}, u32[]{:S(2)}) collective-permute-start(bf16[64,128]{1,0:T(8,128)(2,1)S(1)} %get-tuple-element.32), channel_id=1, source_target_pairs={{0,3},{1,2},{2,1},{3,0},{4,7},{5,6},{6,5},{7,4},{8,11},{9,10},{10,... | collective-permute-start | bytes 49160 | tf_op jit(solution)/shard_map/ppermute | solution.py:468
  19.3 1.3 %collective-permute-start.4 = (bf16[64,128]{1,0:T(8,128)(2,1)S(1)}, bf16[64,128]{1,0:T(8,128)(2,1)S(1)}, u32[]{:S(2)}, u32[]{:S(2)}) collective-permute-start(bf16[64,128]{1,0:T(8,128)(2,1)S(1)} %get-tuple-element.32), channel_id=1, source_target_pairs={{0,2},{1,3},{2,0},{3,1},{4,6},{5,7},{6,4},{7,5},{8,10},{9,11},{10,... | collective-permute-start | bytes 49160 | tf_op jit(solution)/shard_map/ppermute | solution.py:468
  20.7 0.3 collective-permute-start.3
  21.0 1.4 %collective-permute-done.5.refs_3_ = bf16[64,128]{1,0:T(8,128)(2,1)S(1)} collective-permute-done((bf16[64,128]{1,0:T(8,128)(2,1)S(1)}, bf16[64,128]{1,0:T(8,128)(2,1)S(1)}, u32[]{:S(2)}, u32[]{:S(2)}) %collective-permute-start.5) | collective-permute-done | bytes 16416 | tf_op jit(solution)/shard_map/ppermute | solution.py:468
  22.4 0.7 %collective-permute-done.4.refs_2_ = bf16[64,128]{1,0:T(8,128)(2,1)S(1)} collective-permute-done((bf16[64,128]{1,0:T(8,128)(2,1)S(1)}, bf16[64,128]{1,0:T(8,128)(2,1)S(1)}, u32[]{:S(2)}, u32[]{:S(2)}) %collective-permute-start.4) | collective-permute-done | bytes 16416 | tf_op jit(solution)/shard_map/ppermute | solution.py:468
  23.1 0.0 collective-permute-done.3.refs_1_
  23.1 0.0 copy-done.1
  23.1 0.2 expand.1
  23.3 0.1 collective-permute-start.6
  23.4 2.4 %collective-permute-start.7 = (bf16[32,256]{1,0:T(8,128)(2,1)S(1)}, bf16[32,256]{1,0:T(8,128)(2,1)S(1)}, u32[]{:S(2)}, u32[]{:S(2)}) collective-permute-start(bf16[32,256]{1,0:T(8,128)(2,1)S(1)} %get-tuple-element.35), channel_id=1, source_target_pairs={{12,0},{8,4},{4,8},{0,12},{13,1},{9,5},{5,9},{1,13},{14,2},{10,6},... | collective-permute-start | bytes 49160 | tf_op jit(solution)/shard_map/ppermute | solution.py:479
  25.8 1.1 %collective-permute-start.8 = (bf16[32,256]{1,0:T(8,128)(2,1)S(1)}, bf16[32,256]{1,0:T(8,128)(2,1)S(1)}, u32[]{:S(2)}, u32[]{:S(2)}) collective-permute-start(bf16[32,256]{1,0:T(8,128)(2,1)S(1)} %get-tuple-element.36), channel_id=1, source_target_pairs={{4,0},{0,4},{12,8},{8,12},{5,1},{1,5},{13,9},{9,13},{6,2},{2,6},{1... | collective-permute-start | bytes 49160 | tf_op jit(solution)/shard_map/ppermute | solution.py:479
  26.9 1.1 %collective-permute-done.6.refs_0_ = bf16[32,256]{1,0:T(8,128)(2,1)S(1)} collective-permute-done((bf16[32,256]{1,0:T(8,128)(2,1)S(1)}, bf16[32,256]{1,0:T(8,128)(2,1)S(1)}, u32[]{:S(2)}, u32[]{:S(2)}) %collective-permute-start.6) | collective-permute-done | bytes 16416 | tf_op jit(solution)/shard_map/ppermute | solution.py:479
  28.0 1.0 %collective-permute-done.7.refs_1_ = bf16[32,256]{1,0:T(8,128)(2,1)S(1)} collective-permute-done((bf16[32,256]{1,0:T(8,128)(2,1)S(1)}, bf16[32,256]{1,0:T(8,128)(2,1)S(1)}, u32[]{:S(2)}, u32[]{:S(2)}) %collective-permute-start.7) | collective-permute-done | bytes 16416 | tf_op jit(solution)/shard_map/ppermute | solution.py:479
  29.0 0.5 %collective-permute-done.8.refs_2_ = bf16[32,256]{1,0:T(8,128)(2,1)S(1)} collective-permute-done((bf16[32,256]{1,0:T(8,128)(2,1)S(1)}, bf16[32,256]{1,0:T(8,128)(2,1)S(1)}, u32[]{:S(2)}, u32[]{:S(2)}) %collective-permute-start.8) | collective-permute-done | bytes 16416 | tf_op jit(solution)/shard_map/ppermute | solution.py:479
  29.5 1.1 %finish.1 = (bf16[128,256]{1,0:T(8,128)(2,1)}, bf16[128,2048]{1,0:T(8,128)(2,1)}) custom-call(bf16[32,256]{1,0:T(8,128)(2,1)S(1)} %collective-permute-done.6.refs_0_, bf16[32,256]{1,0:T(8,128)(2,1)S(1)} %collective-permute-done.7.refs_1_, bf16[32,256]{1,0:T(8,128)(2,1)S(1)} %collective-permute-done.8.refs_2_, bf16[32,256]{1,0:T(8,128)(2,1)S(1)} %get-tuple-element.37.refs_3_, ...), custom_call_target="tpu_custom_call" | custom-call | tf_op jit(solution)/shard_map/finish/pallas_call | solution.py:483
  (3 shorter events, 0.0 us)
Async XLA Ops:
  2.0 13.4 %collective-permute-start = (bf16[528,128]{1,0:T(8,128)(2,1)S(1)}, bf16[528,128]{1,0:T(8,128)(2,1)S(1)}, u32[]{:S(2)}, u32[]{:S(2)}) collective-permute-start(bf16[528,128]{1,0:T(8,128)(2,1)S(1)} %get-tuple-element.24), channel_id=1, source_target_pairs={{0,12},{4,8},{8,4},{12,0},{1,13},{5,9},{9,5},{13,1},{2,14},{6,10},... | collective-permute-start | bytes 405512 | tf_op jit(solution)/shard_map/ppermute | solution.py:406
  7.1 11.4 %collective-permute-start.1 = (bf16[528,128]{1,0:T(8,128)(2,1)S(1)}, bf16[528,128]{1,0:T(8,128)(2,1)S(1)}, u32[]{:S(2)}, u32[]{:S(2)}) collective-permute-start(bf16[528,128]{1,0:T(8,128)(2,1)S(1)} %get-tuple-element.25), channel_id=1, source_target_pairs={{0,8},{4,12},{8,0},{12,4},{1,9},{5,13},{9,1},{13,5},{2,10},{6,14},... | collective-permute-start | bytes 405512 | tf_op jit(solution)/shard_map/ppermute | solution.py:406
  7.2 11.4 %collective-permute-start.2 = (bf16[528,128]{1,0:T(8,128)(2,1)S(1)}, bf16[528,128]{1,0:T(8,128)(2,1)S(1)}, u32[]{:S(2)}, u32[]{:S(2)}) collective-permute-start(bf16[528,128]{1,0:T(8,128)(2,1)S(1)} %get-tuple-element.26), channel_id=1, source_target_pairs={{0,4},{4,0},{8,12},{12,8},{1,5},{5,1},{9,13},{13,9},{2,6},{6,2},{1... | collective-permute-start | bytes 405512 | tf_op jit(solution)/shard_map/ppermute | solution.py:406
  7.8 10.8 %copy-start = (bf16[4,64,2048]{2,1,0:T(8,128)(2,1)S(1)}, bf16[4,64,2048]{2,1,0:T(8,128)(2,1)}, u32[]{:S(2)}) copy-start(bf16[4,64,2048]{2,1,0:T(8,128)(2,1)} %refs_4_.1) | copy-start | bytes 3145732
  7.8 15.3 %copy-start.1 = (bf16[4,64,256]{2,1,0:T(8,128)(2,1)S(1)}, bf16[4,64,256]{2,1,0:T(8,128)(2,1)}, u32[]{:S(2)}) copy-start(bf16[4,64,256]{2,1,0:T(8,128)(2,1)} %refs_5_.1) | copy-start | bytes 393220
  19.0 3.4 %collective-permute-start.5 = (bf16[64,128]{1,0:T(8,128)(2,1)S(1)}, bf16[64,128]{1,0:T(8,128)(2,1)S(1)}, u32[]{:S(2)}, u32[]{:S(2)}) collective-permute-start(bf16[64,128]{1,0:T(8,128)(2,1)S(1)} %get-tuple-element.32), channel_id=1, source_target_pairs={{0,3},{1,2},{2,1},{3,0},{4,7},{5,6},{6,5},{7,4},{8,11},{9,10},{10,... | collective-permute-start | bytes 49160 | tf_op jit(solution)/shard_map/ppermute | solution.py:468
  19.3 3.7 %collective-permute-start.4 = (bf16[64,128]{1,0:T(8,128)(2,1)S(1)}, bf16[64,128]{1,0:T(8,128)(2,1)S(1)}, u32[]{:S(2)}, u32[]{:S(2)}) collective-permute-start(bf16[64,128]{1,0:T(8,128)(2,1)S(1)} %get-tuple-element.32), channel_id=1, source_target_pairs={{0,2},{1,3},{2,0},{3,1},{4,6},{5,7},{6,4},{7,5},{8,10},{9,11},{10,... | collective-permute-start | bytes 49160 | tf_op jit(solution)/shard_map/ppermute | solution.py:468
  20.7 2.4 %collective-permute-start.3 = (bf16[64,128]{1,0:T(8,128)(2,1)S(1)}, bf16[64,128]{1,0:T(8,128)(2,1)S(1)}, u32[]{:S(2)}, u32[]{:S(2)}) collective-permute-start(bf16[64,128]{1,0:T(8,128)(2,1)S(1)} %get-tuple-element.32), channel_id=1, source_target_pairs={{0,1},{1,0},{2,3},{3,2},{4,5},{5,4},{6,7},{7,6},{8,9},{9,8},{10,11... | collective-permute-start | bytes 49160 | tf_op jit(solution)/shard_map/ppermute | solution.py:468
  23.3 4.7 %collective-permute-start.6 = (bf16[32,256]{1,0:T(8,128)(2,1)S(1)}, bf16[32,256]{1,0:T(8,128)(2,1)S(1)}, u32[]{:S(2)}, u32[]{:S(2)}) collective-permute-start(bf16[32,256]{1,0:T(8,128)(2,1)S(1)} %get-tuple-element.34), channel_id=1, source_target_pairs={{8,0},{12,4},{0,8},{4,12},{9,1},{13,5},{1,9},{5,13},{10,2},{14,6},... | collective-permute-start | bytes 49160 | tf_op jit(solution)/shard_map/ppermute | solution.py:479
  23.4 5.6 %collective-permute-start.7 = (bf16[32,256]{1,0:T(8,128)(2,1)S(1)}, bf16[32,256]{1,0:T(8,128)(2,1)S(1)}, u32[]{:S(2)}, u32[]{:S(2)}) collective-permute-start(bf16[32,256]{1,0:T(8,128)(2,1)S(1)} %get-tuple-element.35), channel_id=1, source_target_pairs={{12,0},{8,4},{4,8},{0,12},{13,1},{9,5},{5,9},{1,13},{14,2},{10,6},... | collective-permute-start | bytes 49160 | tf_op jit(solution)/shard_map/ppermute | solution.py:479
  25.8 3.7 %collective-permute-start.8 = (bf16[32,256]{1,0:T(8,128)(2,1)S(1)}, bf16[32,256]{1,0:T(8,128)(2,1)S(1)}, u32[]{:S(2)}, u32[]{:S(2)}) collective-permute-start(bf16[32,256]{1,0:T(8,128)(2,1)S(1)} %get-tuple-element.36), channel_id=1, source_target_pairs={{4,0},{0,4},{12,8},{8,12},{5,1},{1,5},{13,9},{9,13},{6,2},{2,6},{1... | collective-permute-start | bytes 49160 | tf_op jit(solution)/shard_map/ppermute | solution.py:479
